TPU v7x, 512 devices: a whole 4x8x8 slice. The times are simulated.
512 devices in a mesh: pipe: 32 (over y, x_lo, core), ctx: 16 (over z, x_hi).
Axes of the slice: x: 4 (x_hi: 2, x_lo: 2; x = x_hi * 2 + x_lo), y: 8, z: 8, core: 2. Of those that a mesh axis runs over, the one named last changes fastest.
Arguments:
- queries: bfloat16 [32, 128, 36864], P('pipe', 'ctx')
- out_grad: bfloat16 [32, 128, 32768], P('pipe', 'ctx'), may hold values from -6 to 6
- latent: bfloat16 [32, 2048, 512], P('pipe', 'ctx')
- rope_keys: bfloat16 [32, 2048, 64], P('pipe', 'ctx'), may hold values from -6 to 6
- gain: float32 [16, 512], replicated, may hold values from 0.5 to 2
- block_map: int32 [32, 32], P('pipe', 'ctx'), may hold values from 0 to 31, as said below
- query_start: int32 [32, 16], P('pipe', 'ctx'), may hold values from 64 to 2040, as said below
Outputs:
- attended: bfloat16 [32, 128, 32768], P('pipe', 'ctx')
- query_grad: bfloat16 [32, 128, 36864], P('pipe', 'ctx')
- latent_grad: bfloat16 [32, 2048, 512], P('pipe', 'ctx')
- rope_grad: bfloat16 [32, 2048, 64], P('pipe', 'ctx')
- gain_grad: float32 [32, 512], P('pipe')
Inputs may be any that keep to these rules, and one draw needn't show every extreme that they name: `block_map`: each row is an ordering of the 32 blocks: every block once. Slot t lies on ctx device t // 2. `query_start`: A device's 8 queries lie inside the later, in sequence order, of the two blocks in its slots; the device holding the last block has its queries at that block's end.
All inputs are finite; a program needn't handle non-finite values.
Results may differ from a plain program's by a relative error of at most 0.02.
Values may be sent and summed in bfloat16 or wider, within the bound.
No kernel may reach another device: no remote copies, remote signals or barrier semaphores. Data moves between devices by JAX's collectives and lax.ppermute only.
A program may use at most 64 MiB of HBM per device.

v0:
```python
import math

import jax
import jax.numpy as jnp
from jax import lax
from jax.sharding import PartitionSpec as P

HEADS = 64
DL = 512
DR = 64


score_scale = 1.0 / math.sqrt(192.0)


def from_partner(value, axis, bit):
    mask = 2**bit
    pairs = [(source, source ^ mask) for source in range(lax.axis_size(axis))]
    return lax.ppermute(value, axis, pairs)


def shards(queries, out_grad, latent, rope_keys, gain, block_map, query_start):
    query_len = queries.shape[1]
    width = DL
    key_width = DL + DR
    pipe_size = lax.axis_size("pipe")
    pipe_place = lax.axis_index("pipe")
    section_row = jnp.minimum(pipe_place, pipe_size - 1 - pipe_place)
    gain_row = lax.dynamic_index_in_dim(gain, section_row, 0, keepdims=False)
    latent_f = latent[0].astype(jnp.float32)
    inverse = lax.rsqrt(jnp.mean(latent_f * latent_f, axis=-1, keepdims=True) + 1e-06)
    normal_unit = latent_f * inverse
    local_keys = jnp.concatenate(
        [normal_unit * gain_row[None, :], rope_keys[0].astype(jnp.float32)], axis=1
    ).astype(jnp.bfloat16)
    key_rows, all_blocks = (
        lax.all_gather(local_keys, "ctx", axis=0, tiled=True),
        lax.all_gather(block_map[0], "ctx", axis=0, tiled=True),
    )
    block_len = latent.shape[1] // 2
    key_pos = (
        all_blocks[:, None] * block_len + jnp.arange(block_len, dtype=jnp.int32)[None, :]
    ).reshape(-1)
    query_rows = queries[0].reshape(query_len * HEADS, key_width)
    row_pos = jnp.repeat(query_start[0, 0] + jnp.arange(query_len, dtype=jnp.int32), HEADS)
    scores = (
        lax.dot_general(
            query_rows, key_rows, (((1,), (1,)), ((), ())), preferred_element_type=jnp.float32
        )
        * score_scale
    )
    visible = key_pos[None, :] <= row_pos[:, None]
    scores = jnp.where(visible, scores, -jnp.inf)
    row_max = jnp.max(scores, axis=1, keepdims=True)
    expsum = jnp.exp(scores - row_max)
    weights_f = expsum / jnp.sum(expsum, axis=1, keepdims=True)
    weights_b = weights_f.astype(jnp.bfloat16)
    value_rows = key_rows[:, :width]
    attended = jnp.dot(weights_b, value_rows, preferred_element_type=jnp.float32).astype(
        jnp.bfloat16
    )
    grad_rows = out_grad[0].reshape(query_len * HEADS, width)
    dprob = lax.dot_general(
        grad_rows, value_rows, (((1,), (1,)), ((), ())), preferred_element_type=jnp.float32
    )
    row_delta = jnp.sum(
        grad_rows.astype(jnp.float32) * attended.astype(jnp.float32), axis=1, keepdims=True
    )
    dscore = (weights_f * (dprob - row_delta) * score_scale).astype(jnp.bfloat16)
    query_grad = jnp.dot(dscore, key_rows, preferred_element_type=jnp.float32).astype(jnp.bfloat16)
    score_side = lax.dot_general(
        dscore, query_rows, (((0,), (0,)), ((), ())), preferred_element_type=jnp.float32
    )
    value_side = lax.dot_general(
        weights_b, grad_rows, (((0,), (0,)), ((), ())), preferred_element_type=jnp.float32
    )
    key_grad = lax.psum_scatter(
        (score_side + jnp.pad(value_side, ((0, 0), (0, key_width - width)))).astype(jnp.bfloat16),
        "ctx",
        scatter_dimension=0,
        tiled=True,
    ).astype(jnp.float32)
    g_part = key_grad[:, :width]
    rope_grad = key_grad[:, width:].astype(jnp.bfloat16)
    gated = g_part * gain_row[None, :]
    latent_grad = (
        inverse * gated - latent_f * inverse**3 * jnp.mean(gated * latent_f, axis=-1, keepdims=True)
    ).astype(jnp.bfloat16)
    gain_part = jnp.sum(g_part * normal_unit, axis=0)
    micro_total = lax.psum(gain_part, "ctx")
    mirrored = micro_total
    for bit_index in range(pipe_size.bit_length() - 1):
        mirrored = from_partner(mirrored, "pipe", bit_index)
    gain_grad = micro_total + mirrored
    return (
        attended.reshape(1, query_len, HEADS * width),
        query_grad.reshape(1, query_len, HEADS * key_width),
        latent_grad[None],
        rope_grad[None],
        gain_grad[None],
    )


def solution(mesh):
    return jax.shard_map(
        shards,
        mesh=mesh,
        in_specs=(
            P("pipe", "ctx", None),
            P("pipe", "ctx", None),
            P("pipe", "ctx", None),
            P("pipe", "ctx", None),
            P(),
            P("pipe", "ctx"),
            P("pipe", "ctx"),
        ),
        out_specs=(
            P("pipe", "ctx", None),
            P("pipe", "ctx", None),
            P("pipe", "ctx", None),
            P("pipe", "ctx", None),
            P("pipe", None),
        ),
        check_vma=False,
    )
```

profile of v0, /device:TPU:1, one launch (start us, length us, event | category | flops | bytes accessed | tf_op | source)
XLA Modules:
  0.0 422.6 jit_solution(8649470475273148674)
XLA Ops:
  8.5 1.4 pad_maximum_fusion
  10.8 1.3 dynamic-slice
  13.5 20.5 %all-reduce.1 = s32[32]{0:T(128)S(1)} all-reduce(s32[32]{0:T(128)S(1)} %bitcast_dynamic-update-slice_fusion), channel_id=2, replica_groups=mesh['pipe'=32,'ctx'=16] {'ctx'}, use_global_device_ids=true, to_apply=%add.1 | all-reduce | flops 32 | bytes 256
  34.1 1.3 reshape_squeeze.7
  35.6 1.8 reshape_squeeze.6
  37.5 70.0 %all-gather.3.cloned.1.call-done = bf16[2048,576]{0,1:T(8,128)(2,1)} async-done(((bf16[128,576]{0,1:T(8,128)(2,1)}), bf16[2048,576]{0,1:T(8,128)(2,1)}) %all-gather.3.cloned.1.call-update) | async-done | bytes 2359312 | tf_op jit(solution)/shard_map/all_gather | solution.py:37
  107.5 3.4 fusion.21
  112.3 1.3 fusion.22
  113.9 2.1 multiply_reduce_fusion
  116.0 3.5 fusion.1
  119.4 3.1 add_convert_fusion
  122.6 2.6 copy.24
  125.2 214.4 %reduce-scatter.4.cloned.1.call-done = bf16[128,576]{1,0:T(8,128)(2,1)} async-done(((bf16[2048,576]{1,0:T(8,128)(2,1)}), bf16[128,576]{1,0:T(8,128)(2,1)}) %reduce-scatter.4.cloned.1.call-update) | async-done | bytes 147472
  340.9 31.7 %psum.7 = f32[512]{0:T(512)S(1)} all-reduce(f32[512]{0:T(512)S(1)} %get-tuple-element.20), channel_id=1, replica_groups=mesh['pipe'=32,'ctx'=16] {'ctx'}, use_global_device_ids=true, to_apply=%region_7.8 | all-reduce | flops 512 | bytes 4096 | tf_op jit(solution)/shard_map/psum | solution.py:90
  372.6 13.8 %collective-permute-start = (f32[512]{0:T(512)S(1)}, f32[512]{0:T(512)S(1)}, u32[]{:S(2)}, u32[]{:S(2)}) collective-permute-start(f32[512]{0:T(512)S(1)} %psum.7), channel_id=1, source_target_pairs={{0,16},{16,0},{32,48},{48,32},{64,80},{80,64},{96,112},{112,96},{1... | collective-permute-start | bytes 6152 | tf_op jit(solution)/shard_map/ppermute | solution.py:19
  387.2 2.7 collective-permute-start.1
  389.9 1.6 collective-permute-done.1
  391.5 3.4 collective-permute-start.2
  394.9 3.7 convolution_convert_fusion
  398.9 1.6 reshape.59
  400.7 1.0 reshape.58
  401.8 4.0 collective-permute-start.3
  405.8 1.2 collective-permute-done.3
  407.0 6.1 %collective-permute-start.4 = (f32[512]{0:T(512)S(1)}, f32[512]{0:T(512)S(1)}, u32[]{:S(2)}, u32[]{:S(2)}) collective-permute-start(f32[512]{0:T(512)S(1)} %collective-permute-done.3), channel_id=1, source_target_pairs={{0,256},{16,272},{32,288},{48,304},{64,320},{80,336},{96,352},{112... | collective-permute-start | bytes 6152 | tf_op jit(solution)/shard_map/ppermute | solution.py:19
  (41 shorter events, 9.6 us)
Async XLA Ops:
  7.2 1.2 copy-start
  7.2 100.3 %all-gather.3.cloned.1.call-start = ((), (), s32[]{:S(2)}) async-start(), calls=%async_computation.1 | async-start | bytes 2506752 | tf_op jit(solution)/shard_map/all_gather | solution.py:37
  9.9 329.6 %reduce-scatter.4.cloned.1.call-start = ((), (), s32[]{:S(2)}) async-start(), calls=%async_computation.2 | async-start | bytes 2785280
  112.2 1.7 copy-start.2
  372.6 28.0 %copy-start.1 = (bf16[512,512]{0,1:T(8,128)(2,1)S(1)}, bf16[512,512]{0,1:T(8,128)(2,1)}, u32[]{:S(2)}) copy-start(bf16[512,512]{0,1:T(8,128)(2,1)} %get-tuple-element.27) | copy-start | bytes 1572868
  372.6 14.6 %collective-permute-start = (f32[512]{0:T(512)S(1)}, f32[512]{0:T(512)S(1)}, u32[]{:S(2)}, u32[]{:S(2)}) collective-permute-start(f32[512]{0:T(512)S(1)} %psum.7), channel_id=1, source_target_pairs={{0,16},{16,0},{32,48},{48,32},{64,80},{80,64},{96,112},{112,96},{1... | collective-permute-start | bytes 6152 | tf_op jit(solution)/shard_map/ppermute | solution.py:19
  387.2 4.3 %collective-permute-start.1 = (f32[512]{0:T(512)S(1)}, f32[512]{0:T(512)S(1)}, u32[]{:S(2)}, u32[]{:S(2)}) collective-permute-start(f32[512]{0:T(512)S(1)} %collective-permute-done), channel_id=1, source_target_pairs={{0,32},{16,48},{32,0},{48,16},{64,96},{80,112},{96,64},{112,80},{1... | collective-permute-start | bytes 6152 | tf_op jit(solution)/shard_map/ppermute | solution.py:19
  391.5 10.3 %collective-permute-start.2 = (f32[512]{0:T(512)S(1)}, f32[512]{0:T(512)S(1)}, u32[]{:S(2)}, u32[]{:S(2)}) collective-permute-start(f32[512]{0:T(512)S(1)} %collective-permute-done.1), channel_id=1, source_target_pairs={{0,64},{16,80},{32,96},{48,112},{64,0},{80,16},{96,32},{112,48},{1... | collective-permute-start | bytes 6152 | tf_op jit(solution)/shard_map/ppermute | solution.py:19
  398.6 14.6 %slice-start = ((bf16[128,576]{1,0:T(8,128)(2,1)}), bf16[128,64]{1,0:T(8,128)(2,1)S(1)}, s32[]{:S(2)}) async-start(bf16[128,576]{1,0:T(8,128)(2,1)} %reduce-scatter.4.cloned.1.call-done), calls=%async_computation.3 | async-start | bytes 65536 | tf_op jit(solution)/shard_map/slice | solution.py:84
  401.8 5.2 %collective-permute-start.3 = (f32[512]{0:T(512)S(1)}, f32[512]{0:T(512)S(1)}, u32[]{:S(2)}, u32[]{:S(2)}) collective-permute-start(f32[512]{0:T(512)S(1)} %collective-permute-done.2), channel_id=1, source_target_pairs={{0,128},{16,144},{32,160},{48,176},{64,192},{80,208},{96,224},{112... | collective-permute-start | bytes 6152 | tf_op jit(solution)/shard_map/ppermute | solution.py:19
  407.0 8.2 %collective-permute-start.4 = (f32[512]{0:T(512)S(1)}, f32[512]{0:T(512)S(1)}, u32[]{:S(2)}, u32[]{:S(2)}) collective-permute-start(f32[512]{0:T(512)S(1)} %collective-permute-done.3), channel_id=1, source_target_pairs={{0,256},{16,272},{32,288},{48,304},{64,320},{80,336},{96,352},{112... | collective-permute-start | bytes 6152 | tf_op jit(solution)/shard_map/ppermute | solution.py:19
Sparse Core Ops, SparseCore 0:
  11.6 95.7 all-gather.2
  125.3 214.2 reduce-scatter.3
where the time goes:
time: 426 us; the launch traced here: 423 us
  waiting for transfers between devices  289 us (68%)
  blocking collectives  52.2 us (12%)
  starting transfers between devices  30.1 us (7%)
  matrix products  17.1 us (4%)
  between operations  15.5 us (4%)
  local copies, waits for them, and re-layouts  15.2 us (4%)
    unnamed x3, waiting for transfers between devices  214 us
    all_gather x1, waiting for transfers between devices, shards(): lax.all_gather(local_keys, 'ctx', axis=0, tiled=True)  70 us
    psum x1, blocking collectives, shards(): micro_total = lax.psum(gain_part, 'ctx')  31.7 us
    ppermute x5, starting transfers between devices, from_partner(): return lax.ppermute(value, axis, pairs)  30 us
    unnamed x1, blocking collectives  20.5 us
  transfers between devices with their start and end apart: 7, of which 6 were waited for; matrix products, arithmetic and copies ran while one was open for 3% of the time, Pallas kernels for 0%

commit v1 on v0

v1 whole, which is shorter than its diff:
```python
import math

import jax
import jax.numpy as jnp
from jax import lax
from jax.experimental import pallas as pl
from jax.experimental.pallas import tpu as pltpu
from jax.sharding import Mesh, PartitionSpec as P

HEADS = 64
DL = 512
DR = 64
QKW = DL + DR
WIDE = 640
BLOCK = 64
CHUNK = 256
SCORE_SCALE = 1.0 / math.sqrt(192.0)
F32 = jnp.float32
BF16 = jnp.bfloat16
VMEM = pl.BlockSpec(memory_space=pltpu.VMEM)
SMEM = pl.BlockSpec(memory_space=pltpu.SMEM)


def params():
    return pltpu.CompilerParams(vmem_limit_bytes=48 * 1024 * 1024)


def section_gain(gain_ref, section_ref):
    return gain_ref[pl.ds(section_ref[0], 1), :]


def key_kernel(section_ref, latent_ref, rope_ref, gain_ref, keys_ref):
    latent = latent_ref[...].astype(F32)
    inverse = lax.rsqrt(jnp.mean(latent * latent, axis=-1, keepdims=True) + 1e-06)
    keys_ref[:, :DL] = (latent * inverse * section_gain(gain_ref, section_ref)).astype(BF16)
    keys_ref[:, DL:QKW] = rope_ref[...]
    keys_ref[:, QKW:] = jnp.zeros((keys_ref.shape[0], WIDE - QKW), BF16)


def nt_dot(a, b):
    return lax.dot_general(a, b, (((1,), (1,)), ((), ())), preferred_element_type=F32)


def tn_dot(a, b):
    return lax.dot_general(a, b, (((0,), (0,)), ((), ())), preferred_element_type=F32)


def fold(value, combine):
    parts = [value[i * 8 : (i + 1) * 8] for i in range(value.shape[0] // 8)]
    while len(parts) > 1:
        half = len(parts) // 2
        parts = [combine(parts[i], parts[half + i]) for i in range(half)]
    return parts[0]


def core_kernel(
    blocks_ref, place_ref, q_ref, do_ref, k_ref, kg_ref, w_ref, ds_ref, s_ref, dp_ref
):
    keys, rows = s_ref.shape
    query_start, my_x = place_ref[0], place_ref[1]
    chunks = keys // CHUNK
    groups = CHUNK // BLOCK
    token = lax.broadcasted_iota(jnp.int32, (BLOCK, rows), 1) // HEADS
    lead = lax.broadcasted_iota(jnp.int32, (BLOCK, rows), 0) - token
    top = None
    for c in range(chunks):
        at = pl.ds(c * CHUNK, CHUNK)
        scores = nt_dot(k_ref[at, :], q_ref[...])
        pieces = []
        for g in range(groups):
            room = query_start - blocks_ref[c * groups + g] * BLOCK
            piece = scores[g * BLOCK : (g + 1) * BLOCK] * SCORE_SCALE
            pieces.append(jnp.where(lead <= room, piece, -jnp.inf))
        scores = jnp.concatenate(pieces, axis=0)
        s_ref[at, :] = scores
        part = fold(scores, jnp.maximum)
        top = part if top is None else jnp.maximum(top, part)
    top = jnp.max(top, axis=0, keepdims=True)
    total = jnp.zeros((8, rows), F32)
    pull = jnp.zeros((8, rows), F32)
    for c in range(chunks):
        at = pl.ds(c * CHUNK, CHUNK)
        dprob = nt_dot(k_ref[at, :DL], do_ref[...])
        expo = jnp.exp(s_ref[at, :] - top)
        s_ref[at, :] = expo
        dp_ref[at, :] = dprob
        total = total + fold(expo, jnp.add)
        pull = pull + fold(expo * dprob, jnp.add)
    scale = 1.0 / jnp.sum(total, axis=0, keepdims=True)
    delta = jnp.sum(pull, axis=0, keepdims=True) * scale
    for c in range(chunks):
        at = pl.ds(c * CHUNK, CHUNK)
        weights = s_ref[at, :] * scale
        dscore = (weights * (dp_ref[at, :] - delta) * SCORE_SCALE).astype(BF16)
        weights = weights.astype(BF16)
        w_ref[at, :] = weights
        ds_ref[at, :] = dscore
        lat = jnp.dot(dscore, q_ref[:, :DL], preferred_element_type=F32)
        lat = lat + jnp.dot(weights, do_ref[...], preferred_element_type=F32)
        rope = jnp.dot(dscore, q_ref[:, DL:], preferred_element_type=F32)
        for half in range(2):
            to = pl.ds(pl.multiple_of(c * CHUNK + 128 * (half ^ my_x), 128), 128)
            kg_ref[to, :DL] = lat[half * 128 : half * 128 + 128].astype(BF16)
            kg_ref[to, DL:] = rope[half * 128 : half * 128 + 128].astype(BF16)


def query_kernel(
    section_ref, w_ref, ds_ref, k_ref, q_ref, do_ref, gain_ref, att_ref, dq_ref, part_ref
):
    att = tn_dot(w_ref[...], k_ref[:, :DL])
    dq = tn_dot(ds_ref[...], k_ref[...])
    att_ref[...] = att.astype(BF16)
    dq_ref[...] = dq[:, :QKW].astype(BF16)
    terms = q_ref[:, :DL].astype(F32) * dq[:, :DL] + do_ref[...].astype(F32) * att
    part = jnp.sum(fold(terms, jnp.add), axis=0, keepdims=True)
    part_ref[...] = part / section_gain(gain_ref, section_ref)


def grad_kernel(section_ref, own_ref, far_ref, latent_ref, gain_ref, lg_ref, rg_ref):
    gain = section_gain(gain_ref, section_ref)
    latent = latent_ref[...].astype(F32)
    inverse = lax.rsqrt(jnp.mean(latent * latent, axis=-1, keepdims=True) + 1e-06)
    total = own_ref[...].astype(F32) + far_ref[...].astype(F32)
    gated = total[:, :DL] * gain
    mean = jnp.mean(gated * latent, axis=-1, keepdims=True)
    lg_ref[...] = (inverse * gated - latent * (inverse * inverse * inverse) * mean).astype(BF16)
    rg_ref[...] = total[:, DL:QKW].astype(BF16)


def shards(queries, out_grad, latent, rope_keys, gain, block_map, query_start):
    tokens = queries.shape[1]
    rows = tokens * HEADS
    own = latent.shape[1]
    n_pipe = lax.axis_size("pipe")
    n_z = lax.axis_size("z")
    n_x = lax.axis_size("x")
    keys = own * n_z * n_x
    pipe = lax.axis_index("pipe")
    section = jnp.minimum(pipe, n_pipe - 1 - pipe).reshape(1)
    place = jnp.stack([query_start[0, 0], lax.axis_index("x")])

    local = pl.pallas_call(
        key_kernel,
        out_shape=jax.ShapeDtypeStruct((own, WIDE), BF16),
        in_specs=[SMEM, VMEM, VMEM, VMEM],
        out_specs=VMEM,
        compiler_params=params(),
    )(section, latent[0], rope_keys[0], gain)
    pair = lax.all_gather(local, "x", axis=0, tiled=True)
    key_rows = lax.all_gather(pair, "z", axis=0, tiled=True)
    blocks = lax.all_gather(block_map[0], ("z", "x"), axis=0, tiled=True)

    q = jnp.pad(queries[0].reshape(rows, QKW), ((0, 0), (0, WIDE - QKW)))
    do = out_grad[0].reshape(rows, DL)
    kg, w, ds = pl.pallas_call(
        core_kernel,
        out_shape=(
            jax.ShapeDtypeStruct((keys, WIDE), BF16),
            jax.ShapeDtypeStruct((keys, rows), BF16),
            jax.ShapeDtypeStruct((keys, rows), BF16),
        ),
        in_specs=[SMEM, SMEM, VMEM, VMEM, VMEM],
        out_specs=(VMEM, VMEM, VMEM),
        scratch_shapes=[pltpu.VMEM((keys, rows), F32), pltpu.VMEM((keys, rows), F32)],
        compiler_params=params(),
        cost_estimate=pl.CostEstimate(
            flops=2 * keys * rows * (2 * WIDE + 2 * DL), bytes_accessed=10**7, transcendentals=keys * rows
        ),
    )(blocks, place, q, do, key_rows)
    mine = lax.psum_scatter(kg, "z", scatter_dimension=0, tiled=True)

    att, dq, part = pl.pallas_call(
        query_kernel,
        out_shape=(
            jax.ShapeDtypeStruct((rows, DL), BF16),
            jax.ShapeDtypeStruct((rows, QKW), BF16),
            jax.ShapeDtypeStruct((1, DL), F32),
        ),
        in_specs=[SMEM] + [VMEM] * 6,
        out_specs=(VMEM, VMEM, VMEM),
        compiler_params=params(),
        cost_estimate=pl.CostEstimate(
            flops=2 * keys * rows * (WIDE + DL), bytes_accessed=10**7, transcendentals=0
        ),
    )(section, w, ds, key_rows, q, do, gain)

    def swap(value, axis, mask):
        size = lax.axis_size(axis)
        return lax.ppermute(value, axis, [(i, i ^ mask) for i in range(size)])

    part = part + swap(part, "pipe", n_pipe - 1)
    part = part + swap(part, "x", 1)
    for bit in (1, 2, 4):
        part = part + swap(part, "z", bit)

    far = swap(mine[own:], "x", 1)
    latent_grad, rope_grad = pl.pallas_call(
        grad_kernel,
        out_shape=(
            jax.ShapeDtypeStruct((own, DL), BF16),
            jax.ShapeDtypeStruct((own, DR), BF16),
        ),
        in_specs=[SMEM] + [VMEM] * 4,
        out_specs=(VMEM, VMEM),
        compiler_params=params(),
    )(section, mine[:own], far, latent[0], gain)
    return (
        att.reshape(1, tokens, HEADS * DL),
        dq.reshape(1, tokens, HEADS * QKW),
        latent_grad[None],
        rope_grad[None],
        part,
    )


def solution(mesh):
    n_pipe, n_ctx = mesh.devices.shape
    split = Mesh(mesh.devices.reshape(n_pipe, n_ctx // 2, 2), ("pipe", "z", "x"))
    tokens = P("pipe", ("z", "x"), None)
    ints = P("pipe", ("z", "x"))
    return jax.shard_map(
        shards,
        mesh=split,
        in_specs=(tokens, tokens, tokens, tokens, P(), ints, ints),
        out_specs=(tokens, tokens, tokens, tokens, P("pipe", None)),
        check_vma=False,
    )
```

time: 426 us -> 187 us (0.44)
  the two profiles are of different devices: /device:TPU:1 before, /device:TPU:16 now
where the time goes in v1:
time: 187 us; the launch traced here: 186 us
  waiting for transfers between devices  87 us (47%)
  blocking collectives  32 us (17%)
  starting transfers between devices  20.1 us (11%)
  Pallas kernels  16.4 us (9%)
  between operations  15.5 us (8%)
  local copies, waits for them, and re-layouts  14.7 us (8%)
    reduce_scatter x1, waiting for transfers between devices, shards(): mine = lax.psum_scatter(kg, 'z', scatter_dimension=0, tiled=True)  46 us
    all_gather x1, blocking collectives, shards(): blocks = lax.all_gather(block_map[0], ('z', 'x'), axis=0, tiled=True)  23.6 us
    all_gather x1, waiting for transfers between devices, shards(): key_rows = lax.all_gather(pair, 'z', axis=0, tiled=True)  21.7 us
    ppermute x6, starting transfers between devices, swap(): return lax.ppermute(value, axis, [(i, i ^ mask) for i in range(size)])  20 us
    ppermute x6, waiting for transfers between devices, swap(): return lax.ppermute(value, axis, [(i, i ^ mask) for i in range(size)])  19.3 us
    pallas_call x1, Pallas kernels, shards(): pl.pallas_call(core_kernel, out_shape=(jax.ShapeDtypeStruct((keys, WIDE),...  10.1 us
    unnamed x23, local copies, waits for them, and re-layouts  8.9 us
    all_gather x1, blocking collectives, shards(): pair = lax.all_gather(local, 'x', axis=0, tiled=True)  8.36 us
  transfers between devices with their start and end apart: 8, of which 7 were waited for; matrix products, arithmetic and copies ran while one was open for 4% of the time, Pallas kernels for 3%

profile of v1, /device:TPU:16, one launch (start us, length us, event | category | flops | bytes accessed | tf_op | source)
XLA Modules:
  0.0 186.3 jit_solution(13249333416043889856)
XLA Ops:
  9.9 8.4 %all_gather.10 = bf16[256,640]{1,0:T(8,128)(2,1)} all-gather(bf16[128,640]{1,0:T(8,128)(2,1)S(1)} %shard_map.110), channel_id=1, replica_groups=mesh['pipe'=32,'z'=8,'x'=2] {'x'}, dimensions={0}, use_global_device_ids=true | all-gather | bytes 491520 | tf_op jit(solution)/shard_map/all_gather | solution.py:149
  18.9 1.3 reshape_squeeze.7.do_ref
  21.0 1.3 dynamic-slice
  23.2 23.6 %all-reduce.1.blocks_ref = s32[32]{0:T(128)S(1)} all-reduce(s32[32]{0:T(128)S(1)} %bitcast_dynamic-update-slice_fusion), channel_id=2, replica_groups=mesh['pipe'=32,'z'=8,'x'=2] {'z','x'}, use_global_device_ids=true, to_apply=%add.1 | all-reduce | flops 32 | bytes 256 | tf_op jit(solution)/shard_map/all_gather | solution.py:151
  46.9 21.7 %all-gather.3.cloned.1.call-done.k_ref = bf16[2048,640]{1,0:T(8,128)(2,1)} async-done(((bf16[256,640]{1,0:T(8,128)(2,1)}), bf16[2048,640]{1,0:T(8,128)(2,1)}) %all-gather.3.cloned.1.call-update) | async-done | bytes 2621456 | tf_op jit(solution)/shard_map/all_gather | solution.py:150
  68.5 10.1 %shard_map.111 = (bf16[2048,640]{1,0:T(8,128)(2,1)}, bf16[2048,512]{1,0:T(8,128)(2,1)S(1)}, bf16[2048,512]{1,0:T(8,128)(2,1)S(1)}) custom-call(s32[32]{0:T(128)S(1)} %all-reduce.1.blocks_ref, s32[2]{0:T(128)S(1)} %pad_add_fusion.place_ref, bf16[512,640]{1,0:T(8,128)(2,1)S(1)} %pad.4.q_ref, bf16[512,512]{1,0:T(8,128)(2,1)S(1)} %reshape_squeeze.7.do_ref, ...), custom_call_target="tpu_custom_call" | custom-call | flops 4831838208 | bytes 10000000 | tf_op jit(solution)/shard_map/pallas_call | solution.py:155
  78.6 1.4 copy-done.4
  80.0 1.3 copy-done.6
  81.4 46.0 %reduce-scatter.2.cloned.1.call-done = bf16[256,640]{1,0:T(8,128)(2,1)} async-done(((bf16[2048,640]{1,0:T(8,128)(2,1)}), bf16[256,640]{1,0:T(8,128)(2,1)}) %reduce-scatter.2.cloned.1.call-update) | async-done | bytes 327696 | tf_op jit(solution)/shard_map/reduce_scatter | solution.py:170
  128.4 5.0 %collective-permute-start = (bf16[128,640]{1,0:T(8,128)(2,1)S(1)}, bf16[128,640]{1,0:T(8,128)(2,1)S(1)}, u32[]{:S(2)}, u32[]{:S(2)}) collective-permute-start(bf16[128,640]{1,0:T(8,128)(2,1)S(1)} %get-tuple-element.31), channel_id=1, source_target_pairs={{0,1},{1,0},{2,3},{3,2},{4,5},{5,4},{6,7},{7,6},{8,9},{9,8},{10,11... | collective-permute-start | bytes 491528 | tf_op jit(solution)/shard_map/ppermute | solution.py:189
  133.4 1.6 copy-done.5
  135.0 5.3 %shard_map.112 = (bf16[512,512]{1,0:T(8,128)(2,1)S(1)}, bf16[512,576]{1,0:T(8,128)(2,1)S(1)}, f32[1,512]{1,0:T(1,128)S(1)}) custom-call(s32[1]{0:T(128)} %bitcast.section_ref, bf16[2048,512]{1,0:T(8,128)(2,1)S(1)} %copy-done.5, bf16[2048,512]{1,0:T(8,128)(2,1)} %copy-done.6, bf16[2048,640]{1,0:T(8,128)(2,1)} %all-gather.3.cloned.1.call-done.k_ref, ...), custom_call_target="tpu_custom_call" | custom-call | flops 2415919104 | bytes 10000000 | tf_op jit(solution)/shard_map/pallas_call | solution.py:172
  140.3 1.9 %collective-permute-start.1 = (f32[1,512]{1,0:T(1,128)S(1)}, f32[1,512]{1,0:T(1,128)S(1)}, u32[]{:S(2)}, u32[]{:S(2)}) collective-permute-start(f32[1,512]{1,0:T(1,128)S(1)} %get-tuple-element.20), channel_id=1, source_target_pairs={{0,496},{16,480},{32,464},{48,448},{64,432},{80,416},{96,400},{112... | collective-permute-start | bytes 6152 | tf_op jit(solution)/shard_map/ppermute | solution.py:189
  142.3 6.9 %collective-permute-done.1 = f32[1,512]{1,0:T(1,128)S(1)} collective-permute-done((f32[1,512]{1,0:T(1,128)S(1)}, f32[1,512]{1,0:T(1,128)S(1)}, u32[]{:S(2)}, u32[]{:S(2)}) %collective-permute-start.1) | collective-permute-done | bytes 2080 | tf_op jit(solution)/shard_map/ppermute | solution.py:189
  149.2 2.3 %collective-permute-start.2 = (f32[1,512]{1,0:T(1,128)S(1)}, f32[1,512]{1,0:T(1,128)S(1)}, u32[]{:S(2)}, u32[]{:S(2)}) collective-permute-start(f32[1,512]{1,0:T(1,128)S(1)} %add.19), channel_id=1, source_target_pairs={{0,1},{1,0},{2,3},{3,2},{4,5},{5,4},{6,7},{7,6},{8,9},{9,8},{10,11... | collective-permute-start | bytes 6152 | tf_op jit(solution)/shard_map/ppermute | solution.py:189
  151.5 4.6 %collective-permute-done.2 = f32[1,512]{1,0:T(1,128)S(1)} collective-permute-done((f32[1,512]{1,0:T(1,128)S(1)}, f32[1,512]{1,0:T(1,128)S(1)}, u32[]{:S(2)}, u32[]{:S(2)}) %collective-permute-start.2) | collective-permute-done | bytes 2080 | tf_op jit(solution)/shard_map/ppermute | solution.py:189
  156.1 2.2 %collective-permute-start.3 = (f32[1,512]{1,0:T(1,128)S(1)}, f32[1,512]{1,0:T(1,128)S(1)}, u32[]{:S(2)}, u32[]{:S(2)}) collective-permute-start(f32[1,512]{1,0:T(1,128)S(1)} %add.20), channel_id=1, source_target_pairs={{0,2},{2,0},{4,6},{6,4},{8,10},{10,8},{12,14},{14,12},{1,3},{3,1},... | collective-permute-start | bytes 6152 | tf_op jit(solution)/shard_map/ppermute | solution.py:189
  158.4 3.2 %collective-permute-done.3 = f32[1,512]{1,0:T(1,128)S(1)} collective-permute-done((f32[1,512]{1,0:T(1,128)S(1)}, f32[1,512]{1,0:T(1,128)S(1)}, u32[]{:S(2)}, u32[]{:S(2)}) %collective-permute-start.3) | collective-permute-done | bytes 2080 | tf_op jit(solution)/shard_map/ppermute | solution.py:189
  161.6 3.2 %collective-permute-start.4 = (f32[1,512]{1,0:T(1,128)S(1)}, f32[1,512]{1,0:T(1,128)S(1)}, u32[]{:S(2)}, u32[]{:S(2)}) collective-permute-start(f32[1,512]{1,0:T(1,128)S(1)} %add.21), channel_id=1, source_target_pairs={{0,4},{2,6},{4,0},{6,2},{8,12},{10,14},{12,8},{14,10},{1,5},{3,7},... | collective-permute-start | bytes 6152 | tf_op jit(solution)/shard_map/ppermute | solution.py:189
  164.8 3.2 %collective-permute-done.4 = f32[1,512]{1,0:T(1,128)S(1)} collective-permute-done((f32[1,512]{1,0:T(1,128)S(1)}, f32[1,512]{1,0:T(1,128)S(1)}, u32[]{:S(2)}, u32[]{:S(2)}) %collective-permute-start.4) | collective-permute-done | bytes 2080 | tf_op jit(solution)/shard_map/ppermute | solution.py:189
  168.0 5.3 %collective-permute-start.5 = (f32[1,512]{1,0:T(1,128)S(1)}, f32[1,512]{1,0:T(1,128)S(1)}, u32[]{:S(2)}, u32[]{:S(2)}) collective-permute-start(f32[1,512]{1,0:T(1,128)S(1)} %add.22), channel_id=1, source_target_pairs={{0,8},{2,10},{4,12},{6,14},{8,0},{10,2},{12,4},{14,6},{1,9},{3,11}... | collective-permute-start | bytes 6152 | tf_op jit(solution)/shard_map/ppermute | solution.py:189
  173.3 1.0 reshape.20
  174.3 1.6 reshape.21
  175.9 1.4 collective-permute-done.5
  (35 shorter events, 6.9 us)
Async XLA Ops:
  7.2 15.9 %copy-start.8 = (s32[1,2]{1,0:T(1,128)S(1)}, s32[1,2]{1,0:T(1,128)}, u32[]{:S(2)}) copy-start(s32[1,2]{1,0:T(1,128)} %param.12) | copy-start | bytes 28
  7.2 61.4 %all-gather.3.cloned.1.call-start = ((), (), s32[]{:S(2)}) async-start(), calls=%async_computation.1 | async-start | bytes 2949120 | tf_op jit(solution)/shard_map/all_gather | solution.py:150
  8.1 0.9 copy-start
  9.0 0.8 copy-start.2
  9.7 10.5 %copy-start.7 = (bf16[1,8,36864]{2,1,0:T(8,128)(2,1)S(1)}, bf16[1,8,36864]{2,1,0:T(8,128)(2,1)}, u32[]{:S(2)}) copy-start(bf16[1,8,36864]{2,1,0:T(8,128)(2,1)} %param.7) | copy-start | bytes 1769476
  18.2 109.1 %reduce-scatter.2.cloned.1.call-start = ((), (), s32[]{:S(2)}) async-start(), calls=%async_computation.2 | async-start | bytes 2949120 | tf_op jit(solution)/shard_map/reduce_scatter | solution.py:170
  78.6 1.4 copy-start.4
  80.0 1.3 copy-start.6
  81.4 52.0 %copy-start.3 = (f32[16,512]{1,0:T(8,128)S(1)}, f32[16,512]{1,0:T(8,128)}, u32[]{:S(2)}) copy-start(f32[16,512]{1,0:T(8,128)} %gain_ref.5) | copy-start | bytes 98308
  128.4 49.5 %collective-permute-start = (bf16[128,640]{1,0:T(8,128)(2,1)S(1)}, bf16[128,640]{1,0:T(8,128)(2,1)S(1)}, u32[]{:S(2)}, u32[]{:S(2)}) collective-permute-start(bf16[128,640]{1,0:T(8,128)(2,1)S(1)} %get-tuple-element.31), channel_id=1, source_target_pairs={{0,1},{1,0},{2,3},{3,2},{4,5},{5,4},{6,7},{7,6},{8,9},{9,8},{10,11... | collective-permute-start | bytes 491528 | tf_op jit(solution)/shard_map/ppermute | solution.py:189
  133.4 1.6 copy-start.5
  135.0 43.0 %copy-start.1 = (bf16[1,128,512]{2,1,0:T(8,128)(2,1)S(1)}, bf16[1,128,512]{2,1,0:T(8,128)(2,1)}, u32[]{:S(2)}) copy-start(bf16[1,128,512]{2,1,0:T(8,128)(2,1)} %param.9) | copy-start | bytes 393220
  140.3 8.8 %collective-permute-start.1 = (f32[1,512]{1,0:T(1,128)S(1)}, f32[1,512]{1,0:T(1,128)S(1)}, u32[]{:S(2)}, u32[]{:S(2)}) collective-permute-start(f32[1,512]{1,0:T(1,128)S(1)} %get-tuple-element.20), channel_id=1, source_target_pairs={{0,496},{16,480},{32,464},{48,448},{64,432},{80,416},{96,400},{112... | collective-permute-start | bytes 6152 | tf_op jit(solution)/shard_map/ppermute | solution.py:189
  149.2 7.0 %collective-permute-start.2 = (f32[1,512]{1,0:T(1,128)S(1)}, f32[1,512]{1,0:T(1,128)S(1)}, u32[]{:S(2)}, u32[]{:S(2)}) collective-permute-start(f32[1,512]{1,0:T(1,128)S(1)} %add.19), channel_id=1, source_target_pairs={{0,1},{1,0},{2,3},{3,2},{4,5},{5,4},{6,7},{7,6},{8,9},{9,8},{10,11... | collective-permute-start | bytes 6152 | tf_op jit(solution)/shard_map/ppermute | solution.py:189
  156.1 5.5 %collective-permute-start.3 = (f32[1,512]{1,0:T(1,128)S(1)}, f32[1,512]{1,0:T(1,128)S(1)}, u32[]{:S(2)}, u32[]{:S(2)}) collective-permute-start(f32[1,512]{1,0:T(1,128)S(1)} %add.20), channel_id=1, source_target_pairs={{0,2},{2,0},{4,6},{6,4},{8,10},{10,8},{12,14},{14,12},{1,3},{3,1},... | collective-permute-start | bytes 6152 | tf_op jit(solution)/shard_map/ppermute | solution.py:189
  161.6 6.4 %collective-permute-start.4 = (f32[1,512]{1,0:T(1,128)S(1)}, f32[1,512]{1,0:T(1,128)S(1)}, u32[]{:S(2)}, u32[]{:S(2)}) collective-permute-start(f32[1,512]{1,0:T(1,128)S(1)} %add.21), channel_id=1, source_target_pairs={{0,4},{2,6},{4,0},{6,2},{8,12},{10,14},{12,8},{14,10},{1,5},{3,7},... | collective-permute-start | bytes 6152 | tf_op jit(solution)/shard_map/ppermute | solution.py:189
  168.0 9.4 %collective-permute-start.5 = (f32[1,512]{1,0:T(1,128)S(1)}, f32[1,512]{1,0:T(1,128)S(1)}, u32[]{:S(2)}, u32[]{:S(2)}) collective-permute-start(f32[1,512]{1,0:T(1,128)S(1)} %add.22), channel_id=1, source_target_pairs={{0,8},{2,10},{4,12},{6,14},{8,0},{10,2},{12,4},{14,6},{1,9},{3,11}... | collective-permute-start | bytes 6152 | tf_op jit(solution)/shard_map/ppermute | solution.py:189
Sparse Core Ops, SparseCore 0:
  18.4 50.1 all-gather.2
  81.5 45.8 reduce-scatter.1

commit v2 on v1

v2 whole, which is shorter than its diff:
```python
import math

import jax
import jax.numpy as jnp
from jax import lax
from jax.experimental import pallas as pl
from jax.experimental.pallas import tpu as pltpu
from jax.sharding import Mesh, PartitionSpec as P

HEADS = 64
DL = 512
DR = 64
QKW = DL + DR
WIDE = 640
BLOCK = 64
SCORE_SCALE = 1.0 / math.sqrt(192.0)
F32 = jnp.float32
BF16 = jnp.bfloat16
VMEM = pl.BlockSpec(memory_space=pltpu.VMEM)
SMEM = pl.BlockSpec(memory_space=pltpu.SMEM)


def call(kernel, out, ins, args):
    return pl.pallas_call(
        kernel,
        out_shape=out,
        in_specs=ins,
        out_specs=jax.tree.map(lambda _: VMEM, out),
        compiler_params=pltpu.CompilerParams(vmem_limit_bytes=16 * 1024 * 1024),
        cost_estimate=pl.CostEstimate(flops=1, bytes_accessed=1, transcendentals=0),
    )(*args)


def shape(rows, columns, dtype):
    return jax.ShapeDtypeStruct((rows, columns), dtype)


def nt_dot(a, b):
    return lax.dot_general(a, b, (((1,), (1,)), ((), ())), preferred_element_type=F32)


def tn_dot(a, b):
    return lax.dot_general(a, b, (((0,), (0,)), ((), ())), preferred_element_type=F32)


def mm(a, b):
    return jnp.dot(a, b, preferred_element_type=F32)


def section_gain(gain_ref, section_ref):
    return gain_ref[pl.ds(section_ref[0], 1), :]


def fold(value, combine):
    parts = [value[i * 8 : (i + 1) * 8] for i in range(value.shape[0] // 8)]
    while len(parts) > 1:
        half = len(parts) // 2
        parts = [combine(parts[i], parts[half + i]) for i in range(half)]
    return parts[0]


def key_kernel(section_ref, blocks_ref, latent_ref, rope_ref, gain_ref, keys_ref):
    own = keys_ref.shape[0]
    latent = latent_ref[...].astype(F32)
    inverse = lax.rsqrt(jnp.mean(latent * latent, axis=-1, keepdims=True) + 1e-06)
    keys_ref[:, :DL] = (latent * inverse * section_gain(gain_ref, section_ref)).astype(BF16)
    keys_ref[:, DL:QKW] = rope_ref[...]
    first = lax.broadcasted_iota(jnp.int32, (own, WIDE - QKW), 0) < BLOCK
    blocks = jnp.where(first, blocks_ref[0, 0], blocks_ref[0, 1])
    keys_ref[:, QKW:] = blocks.astype(F32).astype(BF16)


def masked_scores(q_pos, q_ref, k_ref):
    count = k_ref.shape[0]
    scores = nt_dot(k_ref[...], q_ref[...]) * SCORE_SCALE
    place = (lax.broadcasted_iota(jnp.int32, (count, 1), 0) % BLOCK).astype(F32)
    k_pos = k_ref[:, QKW : QKW + 1].astype(F32) * BLOCK + place
    return jnp.where(k_pos <= q_pos, scores, -jnp.inf)


def stats_kernel(first, parts, *refs):
    pos_ref, q_ref, do_ref = refs[:3]
    k_refs = refs[3 : 3 + parts]
    out_ref = refs[-1]
    q_pos = pos_ref[0:1, :]
    scores = [masked_scores(q_pos, q_ref, k_ref) for k_ref in k_refs]
    top = fold(jnp.concatenate([fold(s, jnp.maximum) for s in scores]), jnp.maximum)
    top = jnp.max(top, axis=0, keepdims=True)
    if not first:
        old = refs[3 + parts]
        top = jnp.maximum(top, old[0:1, :])
    total, pull = 0.0, 0.0
    for s, k_ref in zip(scores, k_refs):
        dprob = nt_dot(k_ref[:, :DL], do_ref[...])
        expo = jnp.exp(s - top)
        total = total + fold(expo, jnp.add)
        pull = pull + fold(expo * dprob, jnp.add)
    total = jnp.sum(total, axis=0, keepdims=True)
    pull = jnp.sum(pull, axis=0, keepdims=True)
    if not first:
        shrink = jnp.exp(old[0:1, :] - top)
        total = total + old[1:2, :] * shrink
        pull = pull + old[2:3, :] * shrink
    out_ref[0:1, :] = top
    out_ref[1:2, :] = total
    out_ref[2:3, :] = pull


def weigh(stats_ref, q_pos, q_ref, do_ref, k_ref):
    scale = 1.0 / stats_ref[1:2, :]
    delta = stats_ref[2:3, :] * scale
    scores = masked_scores(q_pos, q_ref, k_ref)
    dprob = nt_dot(k_ref[:, :DL], do_ref[...])
    weights = jnp.exp(scores - stats_ref[0:1, :]) * scale
    dscore = (weights * (dprob - delta) * SCORE_SCALE).astype(BF16)
    return weights.astype(BF16), dscore


def key_grad_kernel(parts, *refs):
    pos_ref, stats_ref, q_ref, do_ref = refs[:4]
    k_refs = refs[4 : 4 + parts]
    kg_refs = refs[4 + parts : 4 + 2 * parts]
    gain_sum = 0.0
    for k_ref, kg_ref in zip(k_refs, kg_refs):
        weights, dscore = weigh(stats_ref, pos_ref[0:1, :], q_ref, do_ref, k_ref)
        lat = mm(dscore, q_ref[:, :DL]) + mm(weights, do_ref[...])
        kg_ref[:, :DL] = lat.astype(BF16)
        kg_ref[:, DL:] = mm(dscore, q_ref[:, DL:]).astype(BF16)
        gain_sum = gain_sum + fold(lat * k_ref[:, :DL].astype(F32), jnp.add)
    refs[-1][...] = gain_sum


def query_side_kernel(parts, first, *refs):
    pos_ref, stats_ref, q_ref, do_ref = refs[:4]
    k_refs = refs[4 : 4 + parts]
    att_ref, dq_ref = refs[-2:]
    att, dq = (0.0, 0.0) if first else (refs[4 + parts][...], refs[5 + parts][...])
    for k_ref in k_refs:
        weights, dscore = weigh(stats_ref, pos_ref[0:1, :], q_ref, do_ref, k_ref)
        att = att + tn_dot(weights, k_ref[:, :DL])
        dq = dq + tn_dot(dscore, k_ref[...])
    att_ref[...] = att.astype(att_ref.dtype)
    dq_ref[...] = dq[:, : dq_ref.shape[1]].astype(dq_ref.dtype)


def spread(vector):
    high = vector.astype(BF16).astype(F32)
    rows = [part[:, i : i + 64] for part in (high, vector - high) for i in range(0, DL, 64)]
    return jnp.concatenate(rows, axis=0).astype(BF16)


def gathered(ref):
    both = ref[0:16, QKW:].astype(F32)
    both = both[0:8] + both[8:16]
    return jnp.concatenate([both[i : i + 1] for i in range(8)], axis=1)


def gain_kernel(section_ref, gain_ref, *refs):
    total = refs[0][...]
    for ref in refs[1:-2]:
        total = total + ref[...]
    vector = jnp.sum(total, axis=0, keepdims=True) / section_gain(gain_ref, section_ref)
    refs[-2][...] = vector
    refs[-1][...] = spread(vector)


def add_kernel(half, here_ref, come_ref, *refs):
    out_ref = refs[-1]
    if half is None:
        out_ref[...] = (here_ref[...].astype(F32) + come_ref[...].astype(F32)).astype(BF16)
    else:
        own = come_ref.shape[0]
        at, rest = pl.ds(half * own, own), pl.ds((1 - half) * own, own)
        out_ref[at, :] = (here_ref[at, :].astype(F32) + come_ref[...].astype(F32)).astype(BF16)
        out_ref[rest, :] = here_ref[rest, :]
    if len(refs) > 1:
        out_ref[0:16, QKW:] = refs[0][...]


def near_kernel(own_ref, right_ref, left_ref, out_ref):
    out_ref[...] = own_ref[...] + gathered(right_ref) + gathered(left_ref)


def total_kernel(
    x_ref, right_ref, left_ref, here_ref, near_ref, across_ref, own_ref, far_ref, sum_ref
):
    own = own_ref.shape[0]
    for ref, place in ((own_ref, x_ref[0]), (far_ref, 1 - x_ref[0])):
        at = pl.ds(pl.multiple_of(place * own, own), own)
        ref[...] = (
            right_ref[at, :].astype(F32) + left_ref[at, :].astype(F32) + here_ref[at, :].astype(F32)
        ).astype(ref.dtype)
    total = near_ref[...] + across_ref[...] + gathered(right_ref) + gathered(left_ref)
    sum_ref[...] = total
    far_ref[0:16, QKW:] = spread(total)


def latent_kernel(section_ref, own_ref, far_ref, latent_ref, gain_ref, sum_ref, lg_ref, rg_ref, gg_ref):
    gain = section_gain(gain_ref, section_ref)
    latent = latent_ref[...].astype(F32)
    inverse = lax.rsqrt(jnp.mean(latent * latent, axis=-1, keepdims=True) + 1e-06)
    total = own_ref[...] + far_ref[...].astype(F32)
    gated = total[:, :DL] * gain
    mean = jnp.mean(gated * latent, axis=-1, keepdims=True)
    lg_ref[...] = (inverse * gated - latent * (inverse * inverse * inverse) * mean).astype(BF16)
    rg_ref[...] = total[:, DL:QKW].astype(BF16)
    gg_ref[...] = sum_ref[...] + gathered(far_ref)


def after(value, *first):
    return lax.optimization_barrier((value, *first))


def swap(value, axis, mask):
    size = lax.axis_size(axis)
    return lax.ppermute(value, axis, [(i, i ^ mask) for i in range(size)])


def shards(queries, out_grad, latent, rope_keys, gain, block_map, query_start):
    tokens = queries.shape[1]
    rows = tokens * HEADS
    own = latent.shape[1]
    n_pipe = lax.axis_size("pipe")
    n_z = lax.axis_size("z")
    pipe = lax.axis_index("pipe")
    section = jnp.minimum(pipe, n_pipe - 1 - pipe).reshape(1)
    place = lax.axis_index("x").reshape(1)

    def right(value):
        return lax.ppermute(value, "z", [(i, (i + 1) % n_z) for i in range(n_z)])

    def left(value):
        return lax.ppermute(value, "z", [(i, (i - 1) % n_z) for i in range(n_z)])

    local = call(
        key_kernel,
        shape(own, WIDE, BF16),
        [SMEM, SMEM, VMEM, VMEM, VMEM],
        (section, block_map, latent[0], rope_keys[0], gain),
    )
    pair = lax.all_gather(local, "x", axis=0, tiled=True)
    q = jnp.pad(queries[0].reshape(rows, QKW), ((0, 0), (0, WIDE - QKW)))
    do = out_grad[0].reshape(rows, DL)
    token = jnp.arange(8 * rows, dtype=jnp.int32).reshape(8, rows) % rows // HEADS
    q_pos = (query_start[0, 0] + token).astype(F32)

    def take_stats(held, stats):
        args = [q_pos, q, do, *held] + ([] if stats is None else [stats])
        return call(
            lambda *refs: stats_kernel(stats is None, len(held), *refs),
            shape(8, rows, F32),
            [VMEM] * len(args),
            args,
        )

    def key_grads(held):
        args = [q_pos, stats, q, do, *held]
        return call(
            lambda *refs: key_grad_kernel(len(held), *refs),
            [shape(piece.shape[0], WIDE, BF16) for piece in held] + [shape(8, DL, F32)],
            [VMEM] * len(args),
            args,
        )

    def query_side(held, sums, last=False):
        args = [q_pos, stats, q, do, *held, *sums]
        dtype = BF16 if last else F32
        return call(
            lambda *refs: query_side_kernel(len(held), not sums, *refs),
            [shape(rows, DL, dtype), shape(rows, QKW if last else WIDE, dtype)],
            [VMEM] * len(args),
            args,
        )

    def add(here, come, half=None, beside=None):
        args = [here, come] + ([] if beside is None else [beside])
        return call(
            lambda *refs: add_kernel(half, *refs),
            shape(*here.shape, BF16),
            [VMEM] * len(args),
            args,
        )

    r1, l1 = right(pair), left(pair)
    r1, q, do = after(r1, q, do)
    r2, l2 = right(r1), left(l1)
    stats = take_stats([pair], None)
    stats = take_stats([r1, l1], stats)
    r2, stats = after(r2, stats)
    r3, l3 = right(r2), left(l2)
    stats = take_stats([r2, l2], stats)
    r3, stats = after(r3, stats)
    r4, l4 = right(r3[:own]), left(l3[own:])
    stats = take_stats([r3, l3], stats)
    stats = take_stats([r4, l4], stats)

    kr4, kl4, g4 = key_grads([r4, l4])
    ahead, behind = right(kr4), left(kl4)
    kr3, kl3, g3 = key_grads([r3, l3])
    ahead, behind = right(add(kl3, ahead, half=0)), left(add(kr3, behind, half=1))
    kr2, kl2, g2 = key_grads([r2, l2])
    kr1, kl1, g1 = key_grads([r1, l1])
    here, g0 = key_grads([pair])
    mine, beside = call(
        gain_kernel,
        [shape(1, DL, F32), shape(16, WIDE - QKW, BF16)],
        [SMEM] + [VMEM] * 6,
        (section, gain, g4, g3, g2, g1, g0),
    )
    ahead = right(add(kl2, ahead, beside=beside))
    behind = left(add(kr2, behind, beside=beside))
    sums = query_side([pair, r1], ())
    near = call(near_kernel, shape(1, DL, F32), [VMEM] * 3, (mine, ahead, behind))
    ahead, *sums = after(ahead, *sums)
    ahead, behind = right(add(kl1, ahead)), left(add(kr1, behind))
    across = swap(near, "z", n_z // 2)
    sums = query_side([l1, r2, l2], sums)
    here, *sums = after(here, *sums)
    mine, other, gain_sum = call(
        total_kernel,
        [shape(own, WIDE, F32), shape(own, WIDE, BF16), shape(1, DL, F32)],
        [SMEM] + [VMEM] * 5,
        (place, ahead, behind, here, near, across),
    )
    other = swap(other, "x", 1)
    att, dq = query_side([r3, l3, r4, l4], sums, last=True)
    other, att, dq = after(other, att, dq)
    latent_grad, rope_grad, gain_sum = call(
        latent_kernel,
        [shape(own, DL, BF16), shape(own, DR, BF16), shape(1, DL, F32)],
        [SMEM] + [VMEM] * 5,
        (section, mine, other, latent[0], gain, gain_sum),
    )
    gain_sum = gain_sum + swap(gain_sum, "pipe", n_pipe - 1)
    return (
        att.reshape(1, tokens, HEADS * DL),
        dq.reshape(1, tokens, HEADS * QKW),
        latent_grad[None],
        rope_grad[None],
        gain_sum,
    )


def solution(mesh):
    n_pipe, n_ctx = mesh.devices.shape
    split = Mesh(mesh.devices.reshape(n_pipe, n_ctx // 2, 2), ("pipe", "z", "x"))
    tokens = P("pipe", ("z", "x"), None)
    ints = P("pipe", ("z", "x"))
    return jax.shard_map(
        shards,
        mesh=split,
        in_specs=(tokens, tokens, tokens, tokens, P(), ints, ints),
        out_specs=(tokens, tokens, tokens, tokens, P("pipe", None)),
        check_vma=False,
    )
```

time: 187 us -> 141 us (0.75)
  the two profiles are of different devices: /device:TPU:16 before, /device:TPU:1 now
where the time goes in v2:
time: 141 us; the launch traced here: 140 us
  starting transfers between devices  84.6 us (60%)
  Pallas kernels  23.7 us (17%)
  local copies, waits for them, and re-layouts  11.2 us (8%)
  waiting for transfers between devices  10.7 us (8%)
  blocking collectives  6.94 us (5%)
  between operations  1.84 us (1%)
    ppermute x8, starting transfers between devices, left(): return lax.ppermute(value, 'z', [(i, (i - 1) % n_z) for i in range(n_z)])  37.3 us
    ppermute x3, starting transfers between devices, swap(): return lax.ppermute(value, axis, [(i, i ^ mask) for i in range(size)])  27 us
    pallas_call x24, Pallas kernels, call(): pl.pallas_call(kernel, out_shape=out, in_specs=ins, out_specs=jax.tree.ma...  23.7 us
    ppermute x8, starting transfers between devices, right(): return lax.ppermute(value, 'z', [(i, (i + 1) % n_z) for i in range(n_z)])  20.2 us
    all_gather x1, blocking collectives, shards(): pair = lax.all_gather(local, 'x', axis=0, tiled=True)  6.94 us
    ppermute x8, waiting for transfers between devices, right(): return lax.ppermute(value, 'z', [(i, (i + 1) % n_z) for i in range(n_z)])  6.75 us
    unnamed x34, local copies, waits for them, and re-layouts  6.42 us
    ppermute x8, waiting for transfers between devices, left(): return lax.ppermute(value, 'z', [(i, (i - 1) % n_z) for i in range(n_z)])  3.99 us
  transfers between devices with their start and end apart: 19, of which 6 were waited for; matrix products, arithmetic and copies ran while one was open for 4% of the time, Pallas kernels for 13%

profile of v2, /device:TPU:1, one launch (start us, length us, event | category | flops | bytes accessed | tf_op | source)
XLA Modules:
  0.0 139.6 jit_solution(16498922945837149519)
XLA Ops:
  4.5 6.9 %all_gather.3.refs_3_.refs_4_ = bf16[256,640]{1,0:T(8,128)(2,1)S(1)} all-gather(bf16[128,640]{1,0:T(8,128)(2,1)S(1)} %shard_map.110), channel_id=1, replica_groups=mesh['pipe'=32,'z'=8,'x'=2] {'x'}, dimensions={0}, use_global_device_ids=true | all-gather | bytes 491520 | tf_op jit(solution)/shard_map/all_gather | solution.py:241
  11.4 5.1 %collective-permute-start = (bf16[256,640]{1,0:T(8,128)(2,1)S(1)}, bf16[256,640]{1,0:T(8,128)(2,1)S(1)}, u32[]{:S(2)}, u32[]{:S(2)}) collective-permute-start(bf16[256,640]{1,0:T(8,128)(2,1)S(1)} %all_gather.3.refs_3_.refs_4_), channel_id=1, source_target_pairs={{0,2},{2,4},{4,6},{6,8},{8,10},{10,12},{12,14},{14,0},{1,3},{3,5},... | collective-permute-start | bytes 983048 | tf_op jit(solution)/shard_map/ppermute | solution.py:230
  16.5 8.6 %collective-permute-start.2 = (bf16[256,640]{1,0:T(8,128)(2,1)S(1)}, bf16[256,640]{1,0:T(8,128)(2,1)S(1)}, u32[]{:S(2)}, u32[]{:S(2)}) collective-permute-start(bf16[256,640]{1,0:T(8,128)(2,1)S(1)} %all_gather.3.refs_3_.refs_4_), channel_id=1, source_target_pairs={{0,14},{2,0},{4,2},{6,4},{8,6},{10,8},{12,10},{14,12},{1,15},{3,1}... | collective-permute-start | bytes 983048 | tf_op jit(solution)/shard_map/ppermute | solution.py:233
  27.3 2.4 %collective-permute-done.refs_3_.refs_4_.refs_5_ = bf16[256,640]{1,0:T(8,128)(2,1)S(1)} collective-permute-done((bf16[256,640]{1,0:T(8,128)(2,1)S(1)}, bf16[256,640]{1,0:T(8,128)(2,1)S(1)}, u32[]{:S(2)}, u32[]{:S(2)}) %collective-permute-start) | collective-permute-done | bytes 327712 | tf_op jit(solution)/shard_map/ppermute | solution.py:230
  30.6 5.3 %collective-permute-start.4 = (bf16[256,640]{1,0:T(8,128)(2,1)S(1)}, bf16[256,640]{1,0:T(8,128)(2,1)S(1)}, u32[]{:S(2)}, u32[]{:S(2)}) collective-permute-start(bf16[256,640]{1,0:T(8,128)(2,1)S(1)} %collective-permute-done.2.refs_4_.refs_5_), channel_id=1, source_target_pairs={{0,14},{2,0},{4,2},{6,4},{8,6},{10,8},{12,10},{14,12},{1,15},{3,1}... | collective-permute-start | bytes 983048 | tf_op jit(solution)/shard_map/ppermute | solution.py:233
  35.9 1.9 %collective-permute-start.1 = (bf16[256,640]{1,0:T(8,128)(2,1)S(1)}, bf16[256,640]{1,0:T(8,128)(2,1)S(1)}, u32[]{:S(2)}, u32[]{:S(2)}) collective-permute-start(bf16[256,640]{1,0:T(8,128)(2,1)S(1)} %collective-permute-done.refs_3_.refs_4_.refs_5_), channel_id=1, source_target_pairs={{0,2},{2,4},{4,6},{6,8},{8,10},{10,12},{12,14},{14,0},{1,3},{3,5},... | collective-permute-start | bytes 983048 | tf_op jit(solution)/shard_map/ppermute | solution.py:230
  40.4 5.3 %collective-permute-start.6 = (bf16[256,640]{1,0:T(8,128)(2,1)S(1)}, bf16[256,640]{1,0:T(8,128)(2,1)S(1)}, u32[]{:S(2)}, u32[]{:S(2)}) collective-permute-start(bf16[256,640]{1,0:T(8,128)(2,1)S(1)} %collective-permute-done.4.refs_4_.refs_5_.refs_6_), channel_id=1, source_target_pairs={{0,14},{2,0},{4,2},{6,4},{8,6},{10,8},{12,10},{14,12},{1,15},{3,1}... | collective-permute-start | bytes 983048 | tf_op jit(solution)/shard_map/ppermute | solution.py:233
  45.7 1.9 %collective-permute-start.3 = (bf16[256,640]{1,0:T(8,128)(2,1)S(1)}, bf16[256,640]{1,0:T(8,128)(2,1)S(1)}, u32[]{:S(2)}, u32[]{:S(2)}) collective-permute-start(bf16[256,640]{1,0:T(8,128)(2,1)S(1)} %collective-permute-done.1.refs_3_.refs_4_.refs_5_), channel_id=1, source_target_pairs={{0,2},{2,4},{4,6},{6,8},{8,10},{10,12},{12,14},{14,0},{1,3},{3,5},... | collective-permute-start | bytes 983048 | tf_op jit(solution)/shard_map/ppermute | solution.py:230
  49.7 5.0 %collective-permute-start.7 = (bf16[128,640]{1,0:T(8,128)(2,1)S(1)}, bf16[128,640]{1,0:T(8,128)(2,1)S(1)}, u32[]{:S(2)}, u32[]{:S(2)}) collective-permute-start(bf16[128,640]{1,0:T(8,128)(2,1)S(1)} %slice.8), channel_id=1, source_target_pairs={{0,14},{2,0},{4,2},{6,4},{8,6},{10,8},{12,10},{14,12},{1,15},{3,1}... | collective-permute-start | bytes 491528 | tf_op jit(solution)/shard_map/ppermute | solution.py:233
  54.8 1.9 %collective-permute-start.5 = (bf16[128,640]{1,0:T(8,128)(2,1)S(1)}, bf16[128,640]{1,0:T(8,128)(2,1)S(1)}, u32[]{:S(2)}, u32[]{:S(2)}) collective-permute-start(bf16[128,640]{1,0:T(8,128)(2,1)S(1)} %slice.6), channel_id=1, source_target_pairs={{0,2},{2,4},{4,6},{6,8},{8,10},{10,12},{12,14},{14,0},{1,3},{3,5},... | collective-permute-start | bytes 491528 | tf_op jit(solution)/shard_map/ppermute | solution.py:230
  57.7 4.4 %collective-permute-done.5.refs_3_.refs_4_.refs_6_ = bf16[128,640]{1,0:T(8,128)(2,1)S(1)} collective-permute-done((bf16[128,640]{1,0:T(8,128)(2,1)S(1)}, bf16[128,640]{1,0:T(8,128)(2,1)S(1)}, u32[]{:S(2)}, u32[]{:S(2)}) %collective-permute-start.5) | collective-permute-done | bytes 163872 | tf_op jit(solution)/shard_map/ppermute | solution.py:230
  64.3 1.9 %collective-permute-start.12 = (bf16[128,640]{1,0:T(8,128)(2,1)S(1)}, bf16[128,640]{1,0:T(8,128)(2,1)S(1)}, u32[]{:S(2)}, u32[]{:S(2)}) collective-permute-start(bf16[128,640]{1,0:T(8,128)(2,1)S(1)} %get-tuple-element.72), channel_id=1, source_target_pairs={{0,14},{2,0},{4,2},{6,4},{8,6},{10,8},{12,10},{14,12},{1,15},{3,1}... | collective-permute-start | bytes 491528 | tf_op jit(solution)/shard_map/ppermute | solution.py:233
  66.2 3.4 %collective-permute-start.8 = (bf16[128,640]{1,0:T(8,128)(2,1)S(1)}, bf16[128,640]{1,0:T(8,128)(2,1)S(1)}, u32[]{:S(2)}, u32[]{:S(2)}) collective-permute-start(bf16[128,640]{1,0:T(8,128)(2,1)S(1)} %get-tuple-element.59), channel_id=1, source_target_pairs={{0,2},{2,4},{4,6},{6,8},{8,10},{10,12},{12,14},{14,0},{1,3},{3,5},... | collective-permute-start | bytes 491528 | tf_op jit(solution)/shard_map/ppermute | solution.py:230
  71.3 3.1 %collective-permute-start.13 = (bf16[256,640]{1,0:T(8,128)(2,1)S(1)}, bf16[256,640]{1,0:T(8,128)(2,1)S(1)}, u32[]{:S(2)}, u32[]{:S(2)}) collective-permute-start(bf16[256,640]{1,0:T(8,128)(2,1)S(1)} %shard_map.126), channel_id=1, source_target_pairs={{0,14},{2,0},{4,2},{6,4},{8,6},{10,8},{12,10},{14,12},{1,15},{3,1}... | collective-permute-start | bytes 983048 | tf_op jit(solution)/shard_map/ppermute | solution.py:233
  74.5 2.2 %collective-permute-start.9 = (bf16[256,640]{1,0:T(8,128)(2,1)S(1)}, bf16[256,640]{1,0:T(8,128)(2,1)S(1)}, u32[]{:S(2)}, u32[]{:S(2)}) collective-permute-start(bf16[256,640]{1,0:T(8,128)(2,1)S(1)} %shard_map.120), channel_id=1, source_target_pairs={{0,2},{2,4},{4,6},{6,8},{8,10},{10,12},{12,14},{14,0},{1,3},{3,5},... | collective-permute-start | bytes 983048 | tf_op jit(solution)/shard_map/ppermute | solution.py:230
  81.1 4.3 %collective-permute-start.14 = (bf16[256,640]{1,0:T(8,128)(2,1)S(1)}, bf16[256,640]{1,0:T(8,128)(2,1)S(1)}, u32[]{:S(2)}, u32[]{:S(2)}) collective-permute-start(bf16[256,640]{1,0:T(8,128)(2,1)S(1)} %shard_map.127), channel_id=1, source_target_pairs={{0,14},{2,0},{4,2},{6,4},{8,6},{10,8},{12,10},{14,12},{1,15},{3,1}... | collective-permute-start | bytes 983048 | tf_op jit(solution)/shard_map/ppermute | solution.py:233
  85.6 1.9 %collective-permute-start.10 = (bf16[256,640]{1,0:T(8,128)(2,1)S(1)}, bf16[256,640]{1,0:T(8,128)(2,1)S(1)}, u32[]{:S(2)}, u32[]{:S(2)}) collective-permute-start(bf16[256,640]{1,0:T(8,128)(2,1)S(1)} %shard_map.123), channel_id=1, source_target_pairs={{0,2},{2,4},{4,6},{6,8},{8,10},{10,12},{12,14},{14,0},{1,3},{3,5},... | collective-permute-start | bytes 983048 | tf_op jit(solution)/shard_map/ppermute | solution.py:230
  91.6 3.7 %collective-permute-start.15 = (bf16[256,640]{1,0:T(8,128)(2,1)}, bf16[256,640]{1,0:T(8,128)(2,1)S(1)}, u32[]{:S(2)}, u32[]{:S(2)}) collective-permute-start(bf16[256,640]{1,0:T(8,128)(2,1)} %shard_map.128), channel_id=1, source_target_pairs={{0,14},{2,0},{4,2},{6,4},{8,6},{10,8},{12,10},{14,12},{1,15},{3,1}... | collective-permute-start | bytes 983048 | tf_op jit(solution)/shard_map/ppermute | solution.py:233
  96.2 1.9 %collective-permute-start.11 = (bf16[256,640]{1,0:T(8,128)(2,1)}, bf16[256,640]{1,0:T(8,128)(2,1)}, u32[]{:S(2)}, u32[]{:S(2)}) collective-permute-start(bf16[256,640]{1,0:T(8,128)(2,1)} %shard_map.125), channel_id=1, source_target_pairs={{0,2},{2,4},{4,6},{6,8},{8,10},{10,12},{12,14},{14,0},{1,3},{3,5},... | collective-permute-start | bytes 983048 | tf_op jit(solution)/shard_map/ppermute | solution.py:230
  98.2 4.0 %collective-permute-start.16 = (f32[1,512]{1,0:T(1,128)S(1)}, f32[1,512]{1,0:T(1,128)S(1)}, u32[]{:S(2)}, u32[]{:S(2)}) collective-permute-start(f32[1,512]{1,0:T(1,128)S(1)} %shard_map.130.near_ref), channel_id=1, source_target_pairs={{0,8},{2,10},{4,12},{6,14},{8,0},{10,2},{12,4},{14,6},{1,9},{3,11}... | collective-permute-start | bytes 6152 | tf_op jit(solution)/shard_map/ppermute | solution.py:216
  104.7 2.6 %shard_map.129 = (f32[512,512]{1,0:T(8,128)S(1)}, f32[512,640]{1,0:T(8,128)S(1)}) custom-call(f32[8,512]{1,0:T(8,128)S(1)} %fusion.3.refs_0_, f32[8,512]{1,0:T(8,128)S(1)} %shard_map.115.refs_1_, bf16[512,640]{1,0:T(8,128)(2,1)S(1)} %pad.4.refs_1_.refs_2_, bf16[512,512]{1,0:T(8,128)(2,1)S(1)} %reshape_squeeze.7.refs_2_.refs_3_, ...), custom_call_target="tpu_custom_call" | custom-call | flops 1 | bytes 1 | tf_op jit(solution)/shard_map/pallas_call | solution.py:24
  108.7 4.8 %collective-permute-start.17 = (bf16[128,640]{1,0:T(8,128)(2,1)S(1)}, bf16[128,640]{1,0:T(8,128)(2,1)S(1)}, u32[]{:S(2)}, u32[]{:S(2)}) collective-permute-start(bf16[128,640]{1,0:T(8,128)(2,1)S(1)} %get-tuple-element.80), channel_id=1, source_target_pairs={{0,1},{1,0},{2,3},{3,2},{4,5},{5,4},{6,7},{7,6},{8,9},{9,8},{10,11... | collective-permute-start | bytes 491528 | tf_op jit(solution)/shard_map/ppermute | solution.py:216
  113.5 3.0 %shard_map.132 = (bf16[512,512]{1,0:T(8,128)(2,1)S(1)}, bf16[512,576]{1,0:T(8,128)(2,1)S(1)}) custom-call(f32[8,512]{1,0:T(8,128)S(1)} %fusion.3.refs_0_, f32[8,512]{1,0:T(8,128)S(1)} %shard_map.115.refs_1_, bf16[512,640]{1,0:T(8,128)(2,1)S(1)} %pad.4.refs_1_.refs_2_, bf16[512,512]{1,0:T(8,128)(2,1)S(1)} %reshape_squeeze.7.refs_2_.refs_3_, ...), custom_call_target="tpu_custom_call" | custom-call | flops 1 | bytes 1 | tf_op jit(solution)/shard_map/pallas_call | solution.py:24
  117.4 18.3 %collective-permute-start.18 = (f32[1,512]{1,0:T(1,128)S(1)}, f32[1,512]{1,0:T(1,128)S(1)}, u32[]{:S(2)}, u32[]{:S(2)}) collective-permute-start(f32[1,512]{1,0:T(1,128)S(1)} %get-tuple-element.92), channel_id=1, source_target_pairs={{0,496},{16,480},{32,464},{48,448},{64,432},{80,416},{96,400},{112... | collective-permute-start | bytes 6152 | tf_op jit(solution)/shard_map/ppermute | solution.py:216
  (82 shorter events, 33.9 us)
Async XLA Ops:
  3.8 22.6 %copy-start.15 = (bf16[1,8,36864]{2,1,0:T(8,128)(2,1)S(1)}, bf16[1,8,36864]{2,1,0:T(8,128)(2,1)}, u32[]{:S(2)}) copy-start(bf16[1,8,36864]{2,1,0:T(8,128)(2,1)} %param.7) | copy-start | bytes 1769476
  11.4 18.3 %collective-permute-start = (bf16[256,640]{1,0:T(8,128)(2,1)S(1)}, bf16[256,640]{1,0:T(8,128)(2,1)S(1)}, u32[]{:S(2)}, u32[]{:S(2)}) collective-permute-start(bf16[256,640]{1,0:T(8,128)(2,1)S(1)} %all_gather.3.refs_3_.refs_4_), channel_id=1, source_target_pairs={{0,2},{2,4},{4,6},{6,8},{8,10},{10,12},{12,14},{14,0},{1,3},{3,5},... | collective-permute-start | bytes 983048 | tf_op jit(solution)/shard_map/ppermute | solution.py:230
  16.5 14.0 %collective-permute-start.2 = (bf16[256,640]{1,0:T(8,128)(2,1)S(1)}, bf16[256,640]{1,0:T(8,128)(2,1)S(1)}, u32[]{:S(2)}, u32[]{:S(2)}) collective-permute-start(bf16[256,640]{1,0:T(8,128)(2,1)S(1)} %all_gather.3.refs_3_.refs_4_), channel_id=1, source_target_pairs={{0,14},{2,0},{4,2},{6,4},{8,6},{10,8},{12,10},{14,12},{1,15},{3,1}... | collective-permute-start | bytes 983048 | tf_op jit(solution)/shard_map/ppermute | solution.py:233
  30.6 9.8 %collective-permute-start.4 = (bf16[256,640]{1,0:T(8,128)(2,1)S(1)}, bf16[256,640]{1,0:T(8,128)(2,1)S(1)}, u32[]{:S(2)}, u32[]{:S(2)}) collective-permute-start(bf16[256,640]{1,0:T(8,128)(2,1)S(1)} %collective-permute-done.2.refs_4_.refs_5_), channel_id=1, source_target_pairs={{0,14},{2,0},{4,2},{6,4},{8,6},{10,8},{12,10},{14,12},{1,15},{3,1}... | collective-permute-start | bytes 983048 | tf_op jit(solution)/shard_map/ppermute | solution.py:233
  35.9 9.8 %collective-permute-start.1 = (bf16[256,640]{1,0:T(8,128)(2,1)S(1)}, bf16[256,640]{1,0:T(8,128)(2,1)S(1)}, u32[]{:S(2)}, u32[]{:S(2)}) collective-permute-start(bf16[256,640]{1,0:T(8,128)(2,1)S(1)} %collective-permute-done.refs_3_.refs_4_.refs_5_), channel_id=1, source_target_pairs={{0,2},{2,4},{4,6},{6,8},{8,10},{10,12},{12,14},{14,0},{1,3},{3,5},... | collective-permute-start | bytes 983048 | tf_op jit(solution)/shard_map/ppermute | solution.py:230
  40.4 9.3 %collective-permute-start.6 = (bf16[256,640]{1,0:T(8,128)(2,1)S(1)}, bf16[256,640]{1,0:T(8,128)(2,1)S(1)}, u32[]{:S(2)}, u32[]{:S(2)}) collective-permute-start(bf16[256,640]{1,0:T(8,128)(2,1)S(1)} %collective-permute-done.4.refs_4_.refs_5_.refs_6_), channel_id=1, source_target_pairs={{0,14},{2,0},{4,2},{6,4},{8,6},{10,8},{12,10},{14,12},{1,15},{3,1}... | collective-permute-start | bytes 983048 | tf_op jit(solution)/shard_map/ppermute | solution.py:233
  45.7 9.0 %collective-permute-start.3 = (bf16[256,640]{1,0:T(8,128)(2,1)S(1)}, bf16[256,640]{1,0:T(8,128)(2,1)S(1)}, u32[]{:S(2)}, u32[]{:S(2)}) collective-permute-start(bf16[256,640]{1,0:T(8,128)(2,1)S(1)} %collective-permute-done.1.refs_3_.refs_4_.refs_5_), channel_id=1, source_target_pairs={{0,2},{2,4},{4,6},{6,8},{8,10},{10,12},{12,14},{14,0},{1,3},{3,5},... | collective-permute-start | bytes 983048 | tf_op jit(solution)/shard_map/ppermute | solution.py:230
  49.7 7.9 %collective-permute-start.7 = (bf16[128,640]{1,0:T(8,128)(2,1)S(1)}, bf16[128,640]{1,0:T(8,128)(2,1)S(1)}, u32[]{:S(2)}, u32[]{:S(2)}) collective-permute-start(bf16[128,640]{1,0:T(8,128)(2,1)S(1)} %slice.8), channel_id=1, source_target_pairs={{0,14},{2,0},{4,2},{6,4},{8,6},{10,8},{12,10},{14,12},{1,15},{3,1}... | collective-permute-start | bytes 491528 | tf_op jit(solution)/shard_map/ppermute | solution.py:233
  54.8 7.3 %collective-permute-start.5 = (bf16[128,640]{1,0:T(8,128)(2,1)S(1)}, bf16[128,640]{1,0:T(8,128)(2,1)S(1)}, u32[]{:S(2)}, u32[]{:S(2)}) collective-permute-start(bf16[128,640]{1,0:T(8,128)(2,1)S(1)} %slice.6), channel_id=1, source_target_pairs={{0,2},{2,4},{4,6},{6,8},{8,10},{10,12},{12,14},{14,0},{1,3},{3,5},... | collective-permute-start | bytes 491528 | tf_op jit(solution)/shard_map/ppermute | solution.py:230
  64.3 6.9 %collective-permute-start.12 = (bf16[128,640]{1,0:T(8,128)(2,1)S(1)}, bf16[128,640]{1,0:T(8,128)(2,1)S(1)}, u32[]{:S(2)}, u32[]{:S(2)}) collective-permute-start(bf16[128,640]{1,0:T(8,128)(2,1)S(1)} %get-tuple-element.72), channel_id=1, source_target_pairs={{0,14},{2,0},{4,2},{6,4},{8,6},{10,8},{12,10},{14,12},{1,15},{3,1}... | collective-permute-start | bytes 491528 | tf_op jit(solution)/shard_map/ppermute | solution.py:233
  66.2 8.2 %collective-permute-start.8 = (bf16[128,640]{1,0:T(8,128)(2,1)S(1)}, bf16[128,640]{1,0:T(8,128)(2,1)S(1)}, u32[]{:S(2)}, u32[]{:S(2)}) collective-permute-start(bf16[128,640]{1,0:T(8,128)(2,1)S(1)} %get-tuple-element.59), channel_id=1, source_target_pairs={{0,2},{2,4},{4,6},{6,8},{8,10},{10,12},{12,14},{14,0},{1,3},{3,5},... | collective-permute-start | bytes 491528 | tf_op jit(solution)/shard_map/ppermute | solution.py:230
  71.3 9.7 %collective-permute-start.13 = (bf16[256,640]{1,0:T(8,128)(2,1)S(1)}, bf16[256,640]{1,0:T(8,128)(2,1)S(1)}, u32[]{:S(2)}, u32[]{:S(2)}) collective-permute-start(bf16[256,640]{1,0:T(8,128)(2,1)S(1)} %shard_map.126), channel_id=1, source_target_pairs={{0,14},{2,0},{4,2},{6,4},{8,6},{10,8},{12,10},{14,12},{1,15},{3,1}... | collective-permute-start | bytes 983048 | tf_op jit(solution)/shard_map/ppermute | solution.py:233
  74.5 11.0 %collective-permute-start.9 = (bf16[256,640]{1,0:T(8,128)(2,1)S(1)}, bf16[256,640]{1,0:T(8,128)(2,1)S(1)}, u32[]{:S(2)}, u32[]{:S(2)}) collective-permute-start(bf16[256,640]{1,0:T(8,128)(2,1)S(1)} %shard_map.120), channel_id=1, source_target_pairs={{0,2},{2,4},{4,6},{6,8},{8,10},{10,12},{12,14},{14,0},{1,3},{3,5},... | collective-permute-start | bytes 983048 | tf_op jit(solution)/shard_map/ppermute | solution.py:230
  81.1 9.7 %collective-permute-start.14 = (bf16[256,640]{1,0:T(8,128)(2,1)S(1)}, bf16[256,640]{1,0:T(8,128)(2,1)S(1)}, u32[]{:S(2)}, u32[]{:S(2)}) collective-permute-start(bf16[256,640]{1,0:T(8,128)(2,1)S(1)} %shard_map.127), channel_id=1, source_target_pairs={{0,14},{2,0},{4,2},{6,4},{8,6},{10,8},{12,10},{14,12},{1,15},{3,1}... | collective-permute-start | bytes 983048 | tf_op jit(solution)/shard_map/ppermute | solution.py:233
  85.6 9.7 %collective-permute-start.10 = (bf16[256,640]{1,0:T(8,128)(2,1)S(1)}, bf16[256,640]{1,0:T(8,128)(2,1)S(1)}, u32[]{:S(2)}, u32[]{:S(2)}) collective-permute-start(bf16[256,640]{1,0:T(8,128)(2,1)S(1)} %shard_map.123), channel_id=1, source_target_pairs={{0,2},{2,4},{4,6},{6,8},{8,10},{10,12},{12,14},{14,0},{1,3},{3,5},... | collective-permute-start | bytes 983048 | tf_op jit(solution)/shard_map/ppermute | solution.py:230
  89.2 8.9 %copy-start.4 = (f32[512,640]{1,0:T(8,128)}, f32[512,640]{1,0:T(8,128)S(1)}, u32[]{:S(2)}) copy-start(f32[512,640]{1,0:T(8,128)S(1)} %get-tuple-element.75.refs_8_) | copy-start | bytes 3932164
  89.3 8.9 %copy-start.6 = (f32[512,512]{1,0:T(8,128)}, f32[512,512]{1,0:T(8,128)S(1)}, u32[]{:S(2)}) copy-start(f32[512,512]{1,0:T(8,128)S(1)} %get-tuple-element.74.refs_7_) | copy-start | bytes 3145732
  91.6 15.7 %collective-permute-start.15 = (bf16[256,640]{1,0:T(8,128)(2,1)}, bf16[256,640]{1,0:T(8,128)(2,1)S(1)}, u32[]{:S(2)}, u32[]{:S(2)}) collective-permute-start(bf16[256,640]{1,0:T(8,128)(2,1)} %shard_map.128), channel_id=1, source_target_pairs={{0,14},{2,0},{4,2},{6,4},{8,6},{10,8},{12,10},{14,12},{1,15},{3,1}... | collective-permute-start | bytes 983048 | tf_op jit(solution)/shard_map/ppermute | solution.py:233
  96.2 11.2 %collective-permute-start.11 = (bf16[256,640]{1,0:T(8,128)(2,1)}, bf16[256,640]{1,0:T(8,128)(2,1)}, u32[]{:S(2)}, u32[]{:S(2)}) collective-permute-start(bf16[256,640]{1,0:T(8,128)(2,1)} %shard_map.125), channel_id=1, source_target_pairs={{0,2},{2,4},{4,6},{6,8},{8,10},{10,12},{12,14},{14,0},{1,3},{3,5},... | collective-permute-start | bytes 983048 | tf_op jit(solution)/shard_map/ppermute | solution.py:230
  98.2 9.2 %collective-permute-start.16 = (f32[1,512]{1,0:T(1,128)S(1)}, f32[1,512]{1,0:T(1,128)S(1)}, u32[]{:S(2)}, u32[]{:S(2)}) collective-permute-start(f32[1,512]{1,0:T(1,128)S(1)} %shard_map.130.near_ref), channel_id=1, source_target_pairs={{0,8},{2,10},{4,12},{6,14},{8,0},{10,2},{12,4},{14,6},{1,9},{3,11}... | collective-permute-start | bytes 6152 | tf_op jit(solution)/shard_map/ppermute | solution.py:216
  104.7 8.8 %copy-start.1 = (bf16[128,640]{1,0:T(8,128)(2,1)S(1)}, bf16[128,640]{1,0:T(8,128)(2,1)}, u32[]{:S(2)}) copy-start(bf16[128,640]{1,0:T(8,128)(2,1)} %copy-done) | copy-start | bytes 491524
  104.7 8.8 %copy-start.3 = (bf16[128,640]{1,0:T(8,128)(2,1)S(1)}, bf16[128,640]{1,0:T(8,128)(2,1)}, u32[]{:S(2)}) copy-start(bf16[128,640]{1,0:T(8,128)(2,1)} %copy-done.2) | copy-start | bytes 491524
  108.7 7.9 %collective-permute-start.17 = (bf16[128,640]{1,0:T(8,128)(2,1)S(1)}, bf16[128,640]{1,0:T(8,128)(2,1)S(1)}, u32[]{:S(2)}, u32[]{:S(2)}) collective-permute-start(bf16[128,640]{1,0:T(8,128)(2,1)S(1)} %get-tuple-element.80), channel_id=1, source_target_pairs={{0,1},{1,0},{2,3},{3,2},{4,5},{5,4},{6,7},{7,6},{8,9},{9,8},{10,11... | collective-permute-start | bytes 491528 | tf_op jit(solution)/shard_map/ppermute | solution.py:216
  117.4 21.6 %collective-permute-start.18 = (f32[1,512]{1,0:T(1,128)S(1)}, f32[1,512]{1,0:T(1,128)S(1)}, u32[]{:S(2)}, u32[]{:S(2)}) collective-permute-start(f32[1,512]{1,0:T(1,128)S(1)} %get-tuple-element.92), channel_id=1, source_target_pairs={{0,496},{16,480},{32,464},{48,448},{64,432},{80,416},{96,400},{112... | collective-permute-start | bytes 6152 | tf_op jit(solution)/shard_map/ppermute | solution.py:216
  (11 other events, 29.2 us)

commit v3 on v2

--- a/solution.py
+++ b/solution.py
@@ -17,16 +17,18 @@
 F32 = jnp.float32
 BF16 = jnp.bfloat16
 VMEM = pl.BlockSpec(memory_space=pltpu.VMEM)
+HBM = pl.BlockSpec(memory_space=pltpu.HBM)
 SMEM = pl.BlockSpec(memory_space=pltpu.SMEM)
 
 
-def call(kernel, out, ins, args):
+def call(kernel, out, ins, args, scratch=(), limit=16):
     return pl.pallas_call(
         kernel,
         out_shape=out,
         in_specs=ins,
         out_specs=jax.tree.map(lambda _: VMEM, out),
-        compiler_params=pltpu.CompilerParams(vmem_limit_bytes=16 * 1024 * 1024),
+        scratch_shapes=scratch,
+        compiler_params=pltpu.CompilerParams(vmem_limit_bytes=limit * 1024 * 1024),
         cost_estimate=pl.CostEstimate(flops=1, bytes_accessed=1, transcendentals=0),
     )(*args)
 
@@ -59,20 +61,31 @@
     return parts[0]
 
 
-def key_kernel(section_ref, blocks_ref, latent_ref, rope_ref, gain_ref, keys_ref):
+def key_kernel(section_ref, blocks_in, latent_in, rope_in, gain_in, keys_ref, *scratch):
+    blocks_ref, latent_ref, rope_ref, gain_ref, sems = scratch
+    copies = [
+        pltpu.make_async_copy(source, target, sems.at[i])
+        for i, (source, target) in enumerate(
+            zip((latent_in, rope_in, gain_in, blocks_in), (latent_ref, rope_ref, gain_ref, blocks_ref))
+        )
+    ]
+    for copy in copies:
+        copy.start()
+    for copy in copies:
+        copy.wait()
     own = keys_ref.shape[0]
     latent = latent_ref[...].astype(F32)
     inverse = lax.rsqrt(jnp.mean(latent * latent, axis=-1, keepdims=True) + 1e-06)
     keys_ref[:, :DL] = (latent * inverse * section_gain(gain_ref, section_ref)).astype(BF16)
-    keys_ref[:, DL:QKW] = rope_ref[...]
+    keys_ref[:, DL:QKW] = rope_ref[...].astype(F32).T.astype(BF16)
     first = lax.broadcasted_iota(jnp.int32, (own, WIDE - QKW), 0) < BLOCK
     blocks = jnp.where(first, blocks_ref[0, 0], blocks_ref[0, 1])
     keys_ref[:, QKW:] = blocks.astype(F32).astype(BF16)
 
 
-def masked_scores(q_pos, q_ref, k_ref):
+def masked_scores(q_pos, q, k_ref):
     count = k_ref.shape[0]
-    scores = nt_dot(k_ref[...], q_ref[...]) * SCORE_SCALE
+    scores = nt_dot(k_ref[...], q) * SCORE_SCALE
     place = (lax.broadcasted_iota(jnp.int32, (count, 1), 0) % BLOCK).astype(F32)
     k_pos = k_ref[:, QKW : QKW + 1].astype(F32) * BLOCK + place
     return jnp.where(k_pos <= q_pos, scores, -jnp.inf)
@@ -83,7 +96,7 @@
     k_refs = refs[3 : 3 + parts]
     out_ref = refs[-1]
     q_pos = pos_ref[0:1, :]
-    scores = [masked_scores(q_pos, q_ref, k_ref) for k_ref in k_refs]
+    scores = [masked_scores(q_pos, q_ref[...], k_ref) for k_ref in k_refs]
     top = fold(jnp.concatenate([fold(s, jnp.maximum) for s in scores]), jnp.maximum)
     top = jnp.max(top, axis=0, keepdims=True)
     if not first:
@@ -106,41 +119,48 @@
     out_ref[2:3, :] = pull
 
 
-def weigh(stats_ref, q_pos, q_ref, do_ref, k_ref):
-    scale = 1.0 / stats_ref[1:2, :]
-    delta = stats_ref[2:3, :] * scale
-    scores = masked_scores(q_pos, q_ref, k_ref)
+def weights_of(stats_ref, pos_ref, q_ref, k_ref):
+    scores = masked_scores(pos_ref[0:1, :], q_ref[...], k_ref)
+    return jnp.exp(scores - stats_ref[0:1, :]) * (1.0 / stats_ref[1:2, :])
+
+
+def dscore_of(weights, stats_ref, do_ref, k_ref):
+    delta = stats_ref[2:3, :] * (1.0 / stats_ref[1:2, :])
     dprob = nt_dot(k_ref[:, :DL], do_ref[...])
-    weights = jnp.exp(scores - stats_ref[0:1, :]) * scale
-    dscore = (weights * (dprob - delta) * SCORE_SCALE).astype(BF16)
-    return weights.astype(BF16), dscore
+    return (weights * (dprob - delta) * SCORE_SCALE).astype(BF16)
 
 
 def key_grad_kernel(parts, *refs):
     pos_ref, stats_ref, q_ref, do_ref = refs[:4]
     k_refs = refs[4 : 4 + parts]
-    kg_refs = refs[4 + parts : 4 + 2 * parts]
+    kg_refs = refs[4 + parts : -1]
+    split = len(kg_refs) // parts
     gain_sum = 0.0
-    for k_ref, kg_ref in zip(k_refs, kg_refs):
-        weights, dscore = weigh(stats_ref, pos_ref[0:1, :], q_ref, do_ref, k_ref)
+    for i, k_ref in enumerate(k_refs):
+        weights = weights_of(stats_ref, pos_ref, q_ref, k_ref)
+        dscore = dscore_of(weights, stats_ref, do_ref, k_ref)
+        weights = weights.astype(BF16)
         lat = mm(dscore, q_ref[:, :DL]) + mm(weights, do_ref[...])
-        kg_ref[:, :DL] = lat.astype(BF16)
-        kg_ref[:, DL:] = mm(dscore, q_ref[:, DL:]).astype(BF16)
+        rope = mm(dscore, q_ref[:, DL:])
+        for j, kg_ref in enumerate(kg_refs[i * split : (i + 1) * split]):
+            at = slice(j * kg_ref.shape[0], (j + 1) * kg_ref.shape[0])
+            kg_ref[:, :DL] = lat[at].astype(BF16)
+            kg_ref[:, DL:] = rope[at].astype(BF16)
         gain_sum = gain_sum + fold(lat * k_ref[:, :DL].astype(F32), jnp.add)
     refs[-1][...] = gain_sum
 
 
-def query_side_kernel(parts, first, *refs):
+def query_side_kernel(*refs):
     pos_ref, stats_ref, q_ref, do_ref = refs[:4]
-    k_refs = refs[4 : 4 + parts]
     att_ref, dq_ref = refs[-2:]
-    att, dq = (0.0, 0.0) if first else (refs[4 + parts][...], refs[5 + parts][...])
-    for k_ref in k_refs:
-        weights, dscore = weigh(stats_ref, pos_ref[0:1, :], q_ref, do_ref, k_ref)
-        att = att + tn_dot(weights, k_ref[:, :DL])
+    att, dq = 0.0, 0.0
+    for k_ref in refs[4:-2]:
+        weights = weights_of(stats_ref, pos_ref, q_ref, k_ref)
+        dscore = dscore_of(weights, stats_ref, do_ref, k_ref)
+        att = att + tn_dot(weights.astype(BF16), k_ref[:, :DL])
         dq = dq + tn_dot(dscore, k_ref[...])
-    att_ref[...] = att.astype(att_ref.dtype)
-    dq_ref[...] = dq[:, : dq_ref.shape[1]].astype(dq_ref.dtype)
+    att_ref[...] = att
+    dq_ref[...] = dq[:, :QKW]
 
 
 def spread(vector):
@@ -203,7 +223,7 @@
     gated = total[:, :DL] * gain
     mean = jnp.mean(gated * latent, axis=-1, keepdims=True)
     lg_ref[...] = (inverse * gated - latent * (inverse * inverse * inverse) * mean).astype(BF16)
-    rg_ref[...] = total[:, DL:QKW].astype(BF16)
+    rg_ref[...] = total[:, DL:QKW].T.astype(BF16)
     gg_ref[...] = sum_ref[...] + gathered(far_ref)
 
 
@@ -235,8 +255,16 @@
     local = call(
         key_kernel,
         shape(own, WIDE, BF16),
-        [SMEM, SMEM, VMEM, VMEM, VMEM],
-        (section, block_map, latent[0], rope_keys[0], gain),
+        [SMEM, HBM, HBM, HBM, HBM],
+        (section, block_map, latent[0], rope_keys[0].T, gain),
+        [
+            pltpu.SMEM(block_map.shape, jnp.int32),
+            pltpu.VMEM((own, DL), BF16),
+            pltpu.VMEM((DR, own), BF16),
+            pltpu.VMEM(gain.shape, F32),
+            pltpu.SemaphoreType.DMA((4,)),
+        ],
+        limit=60,
     )
     pair = lax.all_gather(local, "x", axis=0, tiled=True)
     q = jnp.pad(queries[0].reshape(rows, QKW), ((0, 0), (0, WIDE - QKW)))
@@ -253,24 +281,20 @@
             args,
         )
 
-    def key_grads(held):
+    def key_grads(held, split=1):
         args = [q_pos, stats, q, do, *held]
+        sizes = [piece.shape[0] // split for piece in held for _ in range(split)]
         return call(
             lambda *refs: key_grad_kernel(len(held), *refs),
-            [shape(piece.shape[0], WIDE, BF16) for piece in held] + [shape(8, DL, F32)],
+            [shape(size, WIDE, BF16) for size in sizes] + [shape(8, DL, F32)],
             [VMEM] * len(args),
             args,
         )
 
-    def query_side(held, sums, last=False):
-        args = [q_pos, stats, q, do, *held, *sums]
-        dtype = BF16 if last else F32
-        return call(
-            lambda *refs: query_side_kernel(len(held), not sums, *refs),
-            [shape(rows, DL, dtype), shape(rows, QKW if last else WIDE, dtype)],
-            [VMEM] * len(args),
-            args,
-        )
+    def query_side(held):
+        args = [q_pos, stats, q, do, *held]
+        out = [shape(rows, DL, F32), shape(rows, QKW, F32)]
+        return call(query_side_kernel, out, [VMEM] * len(args), args)
 
     def add(here, come, half=None, beside=None):
         args = [here, come] + ([] if beside is None else [beside])
@@ -309,13 +333,11 @@
     )
     ahead = right(add(kl2, ahead, beside=beside))
     behind = left(add(kr2, behind, beside=beside))
-    sums = query_side([pair, r1], ())
+    first = query_side([pair, r1, l1, r2])
     near = call(near_kernel, shape(1, DL, F32), [VMEM] * 3, (mine, ahead, behind))
-    ahead, *sums = after(ahead, *sums)
+    ahead, *first = after(ahead, *first)
     ahead, behind = right(add(kl1, ahead)), left(add(kr1, behind))
     across = swap(near, "z", n_z // 2)
-    sums = query_side([l1, r2, l2], sums)
-    here, *sums = after(here, *sums)
     mine, other, gain_sum = call(
         total_kernel,
         [shape(own, WIDE, F32), shape(own, WIDE, BF16), shape(1, DL, F32)],
@@ -323,20 +345,19 @@
         (place, ahead, behind, here, near, across),
     )
     other = swap(other, "x", 1)
-    att, dq = query_side([r3, l3, r4, l4], sums, last=True)
-    other, att, dq = after(other, att, dq)
+    second = query_side([l2, r3, l3, r4, l4])
+    other, *second = after(other, *second)
     latent_grad, rope_grad, gain_sum = call(
         latent_kernel,
-        [shape(own, DL, BF16), shape(own, DR, BF16), shape(1, DL, F32)],
+        [shape(own, DL, BF16), shape(DR, own, BF16), shape(1, DL, F32)],
         [SMEM] + [VMEM] * 5,
         (section, mine, other, latent[0], gain, gain_sum),
     )
     gain_sum = gain_sum + swap(gain_sum, "pipe", n_pipe - 1)
     return (
-        att.reshape(1, tokens, HEADS * DL),
-        dq.reshape(1, tokens, HEADS * QKW),
+        *((a + b).astype(BF16).reshape(1, tokens, -1) for a, b in zip(first, second)),
         latent_grad[None],
-        rope_grad[None],
+        rope_grad.T[None],
         gain_sum,
     )
 

time: 141 us -> 134 us (0.950)
  local copies, waits for them, and re-layouts: 11.2 us -> 4.87 us
    unnamed x34 -> x18, local copies, waits for them, and re-layouts: 6.42 us -> 0.04 us
    ppermute x3, waiting for transfers between devices: 0.01 us -> 4.34 us  [swap(): return lax.ppermute(value, axis, [(i, i ^ mask) for i in range(size)])]
    ppermute x8, starting transfers between devices: 37.3 us -> 41 us  [left(): return lax.ppermute(value, 'z', [(i, (i - 1) % n_z) for i in range(n_z)])]
    ppermute x3, starting transfers between devices: 27 us -> 23.7 us  [swap(): return lax.ppermute(value, axis, [(i, i ^ mask) for i in range(size)])]
    ppermute x8, waiting for transfers between devices: 3.99 us -> 1.31 us  [left(): return lax.ppermute(value, 'z', [(i, (i - 1) % n_z) for i in range(n_z)])]
    ppermute x8, starting transfers between devices: 20.2 us -> 18.7 us  [right(): return lax.ppermute(value, 'z', [(i, (i + 1) % n_z) for i in range(n_z)])]
    pallas_call x24 -> x23, Pallas kernels: 23.7 us -> 23.9 us  [call(): pl.pallas_call(kernel, out_shape=out, in_specs=ins, out_specs=jax.tree.ma...]
  transfers between devices with their start and end apart: 19 -> 19, of which waited for: 6 -> 5; matrix products, arithmetic and copies ran while one was open for 4% -> 4% of each run, Pallas kernels for 13% -> 14%
where the time goes in v3:
time: 134 us; the launch traced here: 133 us
  starting transfers between devices  83.4 us (62%)
  Pallas kernels  23.9 us (18%)
  waiting for transfers between devices  11 us (8%)
  blocking collectives  7.21 us (5%)
  local copies, waits for them, and re-layouts  4.87 us (4%)
  between operations  1.79 us (1%)
    ppermute x8, starting transfers between devices, left(): return lax.ppermute(value, 'z', [(i, (i - 1) % n_z) for i in range(n_z)])  41 us
    pallas_call x23, Pallas kernels, call(): pl.pallas_call(kernel, out_shape=out, in_specs=ins, out_specs=jax.tree.ma...  23.9 us
    ppermute x3, starting transfers between devices, swap(): return lax.ppermute(value, axis, [(i, i ^ mask) for i in range(size)])  23.7 us
    ppermute x8, starting transfers between devices, right(): return lax.ppermute(value, 'z', [(i, (i + 1) % n_z) for i in range(n_z)])  18.7 us
    all_gather x1, blocking collectives, shards(): pair = lax.all_gather(local, 'x', axis=0, tiled=True)  7.21 us
    ppermute x8, waiting for transfers between devices, right(): return lax.ppermute(value, 'z', [(i, (i + 1) % n_z) for i in range(n_z)])  5.34 us
    ppermute x3, waiting for transfers between devices, swap(): return lax.ppermute(value, axis, [(i, i ^ mask) for i in range(size)])  4.34 us
  transfers between devices with their start and end apart: 19, of which 5 were waited for; matrix products, arithmetic and copies ran while one was open for 4% of the time, Pallas kernels for 14%

profile of v3, /device:TPU:1, one launch (start us, length us, event | category | flops | bytes accessed | tf_op | source)
XLA Modules:
  0.0 133.2 jit_solution(5625027443063914097)
XLA Ops:
  2.5 7.2 %all_gather.3.refs_3_.refs_4_ = bf16[256,640]{1,0:T(8,128)(2,1)S(1)} all-gather(bf16[128,640]{1,0:T(8,128)(2,1)} %shard_map.110), channel_id=1, replica_groups=mesh['pipe'=32,'z'=8,'x'=2] {'x'}, dimensions={0}, use_global_device_ids=true | all-gather | bytes 491520 | tf_op jit(solution)/shard_map/all_gather | solution.py:269
  9.7 5.1 %collective-permute-start = (bf16[256,640]{1,0:T(8,128)(2,1)S(1)}, bf16[256,640]{1,0:T(8,128)(2,1)S(1)}, u32[]{:S(2)}, u32[]{:S(2)}) collective-permute-start(bf16[256,640]{1,0:T(8,128)(2,1)S(1)} %all_gather.3.refs_3_.refs_4_), channel_id=1, source_target_pairs={{0,2},{2,4},{4,6},{6,8},{8,10},{10,12},{12,14},{14,0},{1,3},{3,5},... | collective-permute-start | bytes 983048 | tf_op jit(solution)/shard_map/ppermute | solution.py:250
  14.8 8.6 %collective-permute-start.2 = (bf16[256,640]{1,0:T(8,128)(2,1)S(1)}, bf16[256,640]{1,0:T(8,128)(2,1)S(1)}, u32[]{:S(2)}, u32[]{:S(2)}) collective-permute-start(bf16[256,640]{1,0:T(8,128)(2,1)S(1)} %all_gather.3.refs_3_.refs_4_), channel_id=1, source_target_pairs={{0,14},{2,0},{4,2},{6,4},{8,6},{10,8},{12,10},{14,12},{1,15},{3,1}... | collective-permute-start | bytes 983048 | tf_op jit(solution)/shard_map/ppermute | solution.py:253
  25.5 2.3 %collective-permute-done.refs_3_.refs_4_.refs_5_ = bf16[256,640]{1,0:T(8,128)(2,1)S(1)} collective-permute-done((bf16[256,640]{1,0:T(8,128)(2,1)S(1)}, bf16[256,640]{1,0:T(8,128)(2,1)S(1)}, u32[]{:S(2)}, u32[]{:S(2)}) %collective-permute-start) | collective-permute-done | bytes 327712 | tf_op jit(solution)/shard_map/ppermute | solution.py:250
  27.9 1.9 %collective-permute-start.1 = (bf16[256,640]{1,0:T(8,128)(2,1)S(1)}, bf16[256,640]{1,0:T(8,128)(2,1)S(1)}, u32[]{:S(2)}, u32[]{:S(2)}) collective-permute-start(bf16[256,640]{1,0:T(8,128)(2,1)S(1)} %collective-permute-done.refs_3_.refs_4_.refs_5_), channel_id=1, source_target_pairs={{0,2},{2,4},{4,6},{6,8},{8,10},{10,12},{12,14},{14,0},{1,3},{3,5},... | collective-permute-start | bytes 983048 | tf_op jit(solution)/shard_map/ppermute | solution.py:250
  29.8 4.6 %collective-permute-start.4 = (bf16[256,640]{1,0:T(8,128)(2,1)S(1)}, bf16[256,640]{1,0:T(8,128)(2,1)S(1)}, u32[]{:S(2)}, u32[]{:S(2)}) collective-permute-start(bf16[256,640]{1,0:T(8,128)(2,1)S(1)} %collective-permute-done.2.refs_4_.refs_5_.refs_6_), channel_id=1, source_target_pairs={{0,14},{2,0},{4,2},{6,4},{8,6},{10,8},{12,10},{14,12},{1,15},{3,1}... | collective-permute-start | bytes 983048 | tf_op jit(solution)/shard_map/ppermute | solution.py:253
  38.0 1.9 %collective-permute-start.3 = (bf16[256,640]{1,0:T(8,128)(2,1)S(1)}, bf16[256,640]{1,0:T(8,128)(2,1)S(1)}, u32[]{:S(2)}, u32[]{:S(2)}) collective-permute-start(bf16[256,640]{1,0:T(8,128)(2,1)S(1)} %collective-permute-done.1.refs_3_.refs_4_.refs_7_), channel_id=1, source_target_pairs={{0,2},{2,4},{4,6},{6,8},{8,10},{10,12},{12,14},{14,0},{1,3},{3,5},... | collective-permute-start | bytes 983048 | tf_op jit(solution)/shard_map/ppermute | solution.py:250
  39.9 4.6 %collective-permute-start.6 = (bf16[256,640]{1,0:T(8,128)(2,1)S(1)}, bf16[256,640]{1,0:T(8,128)(2,1)S(1)}, u32[]{:S(2)}, u32[]{:S(2)}) collective-permute-start(bf16[256,640]{1,0:T(8,128)(2,1)S(1)} %collective-permute-done.4.refs_4_.refs_5_), channel_id=1, source_target_pairs={{0,14},{2,0},{4,2},{6,4},{8,6},{10,8},{12,10},{14,12},{1,15},{3,1}... | collective-permute-start | bytes 983048 | tf_op jit(solution)/shard_map/ppermute | solution.py:253
  47.0 1.9 %collective-permute-start.5 = (bf16[128,640]{1,0:T(8,128)(2,1)S(1)}, bf16[128,640]{1,0:T(8,128)(2,1)S(1)}, u32[]{:S(2)}, u32[]{:S(2)}) collective-permute-start(bf16[128,640]{1,0:T(8,128)(2,1)S(1)} %slice.6), channel_id=1, source_target_pairs={{0,2},{2,4},{4,6},{6,8},{8,10},{10,12},{12,14},{14,0},{1,3},{3,5},... | collective-permute-start | bytes 491528 | tf_op jit(solution)/shard_map/ppermute | solution.py:250
  49.0 4.6 %collective-permute-start.7 = (bf16[128,640]{1,0:T(8,128)(2,1)S(1)}, bf16[128,640]{1,0:T(8,128)(2,1)S(1)}, u32[]{:S(2)}, u32[]{:S(2)}) collective-permute-start(bf16[128,640]{1,0:T(8,128)(2,1)S(1)} %slice.8), channel_id=1, source_target_pairs={{0,14},{2,0},{4,2},{6,4},{8,6},{10,8},{12,10},{14,12},{1,15},{3,1}... | collective-permute-start | bytes 491528 | tf_op jit(solution)/shard_map/ppermute | solution.py:253
  58.1 1.9 %collective-permute-start.8 = (bf16[128,640]{1,0:T(8,128)(2,1)S(1)}, bf16[128,640]{1,0:T(8,128)(2,1)S(1)}, u32[]{:S(2)}, u32[]{:S(2)}) collective-permute-start(bf16[128,640]{1,0:T(8,128)(2,1)S(1)} %get-tuple-element.53), channel_id=1, source_target_pairs={{0,2},{2,4},{4,6},{6,8},{8,10},{10,12},{12,14},{14,0},{1,3},{3,5},... | collective-permute-start | bytes 491528 | tf_op jit(solution)/shard_map/ppermute | solution.py:250
  60.0 5.0 %collective-permute-start.12 = (bf16[128,640]{1,0:T(8,128)(2,1)S(1)}, bf16[128,640]{1,0:T(8,128)(2,1)S(1)}, u32[]{:S(2)}, u32[]{:S(2)}) collective-permute-start(bf16[128,640]{1,0:T(8,128)(2,1)S(1)} %get-tuple-element.68), channel_id=1, source_target_pairs={{0,14},{2,0},{4,2},{6,4},{8,6},{10,8},{12,10},{14,12},{1,15},{3,1}... | collective-permute-start | bytes 491528 | tf_op jit(solution)/shard_map/ppermute | solution.py:253
  66.7 1.9 %collective-permute-start.9 = (bf16[256,640]{1,0:T(8,128)(2,1)S(1)}, bf16[256,640]{1,0:T(8,128)(2,1)S(1)}, u32[]{:S(2)}, u32[]{:S(2)}) collective-permute-start(bf16[256,640]{1,0:T(8,128)(2,1)S(1)} %shard_map.119), channel_id=1, source_target_pairs={{0,2},{2,4},{4,6},{6,8},{8,10},{10,12},{12,14},{14,0},{1,3},{3,5},... | collective-permute-start | bytes 983048 | tf_op jit(solution)/shard_map/ppermute | solution.py:250
  68.7 4.6 %collective-permute-start.13 = (bf16[256,640]{1,0:T(8,128)(2,1)S(1)}, bf16[256,640]{1,0:T(8,128)(2,1)S(1)}, u32[]{:S(2)}, u32[]{:S(2)}) collective-permute-start(bf16[256,640]{1,0:T(8,128)(2,1)S(1)} %shard_map.126), channel_id=1, source_target_pairs={{0,14},{2,0},{4,2},{6,4},{8,6},{10,8},{12,10},{14,12},{1,15},{3,1}... | collective-permute-start | bytes 983048 | tf_op jit(solution)/shard_map/ppermute | solution.py:253
  77.8 2.1 %collective-permute-start.10 = (bf16[256,640]{1,0:T(8,128)(2,1)S(1)}, bf16[256,640]{1,0:T(8,128)(2,1)S(1)}, u32[]{:S(2)}, u32[]{:S(2)}) collective-permute-start(bf16[256,640]{1,0:T(8,128)(2,1)S(1)} %shard_map.123), channel_id=1, source_target_pairs={{0,2},{2,4},{4,6},{6,8},{8,10},{10,12},{12,14},{14,0},{1,3},{3,5},... | collective-permute-start | bytes 983048 | tf_op jit(solution)/shard_map/ppermute | solution.py:250
  80.1 4.6 %collective-permute-start.14 = (bf16[256,640]{1,0:T(8,128)(2,1)S(1)}, bf16[256,640]{1,0:T(8,128)(2,1)S(1)}, u32[]{:S(2)}, u32[]{:S(2)}) collective-permute-start(bf16[256,640]{1,0:T(8,128)(2,1)S(1)} %shard_map.127), channel_id=1, source_target_pairs={{0,14},{2,0},{4,2},{6,4},{8,6},{10,8},{12,10},{14,12},{1,15},{3,1}... | collective-permute-start | bytes 983048 | tf_op jit(solution)/shard_map/ppermute | solution.py:253
  84.6 3.5 %shard_map.124 = (f32[512,512]{1,0:T(8,128)S(1)}, f32[512,576]{1,0:T(8,128)S(1)}) custom-call(f32[8,512]{1,0:T(8,128)S(1)} %fusion.3.refs_0_, f32[8,512]{1,0:T(8,128)S(1)} %shard_map.115.refs_1_, bf16[512,640]{1,0:T(8,128)(2,1)S(1)} %pad.4.refs_1_.refs_2_, bf16[512,512]{1,0:T(8,128)(2,1)S(1)} %reshape_squeeze.7.refs_2_.refs_3_, ...), custom_call_target="tpu_custom_call" | custom-call | flops 1 | bytes 1 | tf_op jit(solution)/shard_map/pallas_call | solution.py:25
  89.0 1.9 %collective-permute-start.11 = (bf16[256,640]{1,0:T(8,128)(2,1)}, bf16[256,640]{1,0:T(8,128)(2,1)S(1)}, u32[]{:S(2)}, u32[]{:S(2)}) collective-permute-start(bf16[256,640]{1,0:T(8,128)(2,1)} %shard_map.125), channel_id=1, source_target_pairs={{0,2},{2,4},{4,6},{6,8},{8,10},{10,12},{12,14},{14,0},{1,3},{3,5},... | collective-permute-start | bytes 983048 | tf_op jit(solution)/shard_map/ppermute | solution.py:250
  91.8 4.6 %collective-permute-start.15 = (bf16[256,640]{1,0:T(8,128)(2,1)}, bf16[256,640]{1,0:T(8,128)(2,1)S(1)}, u32[]{:S(2)}, u32[]{:S(2)}) collective-permute-start(bf16[256,640]{1,0:T(8,128)(2,1)} %shard_map.128), channel_id=1, source_target_pairs={{0,14},{2,0},{4,2},{6,4},{8,6},{10,8},{12,10},{14,12},{1,15},{3,1}... | collective-permute-start | bytes 983048 | tf_op jit(solution)/shard_map/ppermute | solution.py:253
  96.4 4.0 %collective-permute-start.16 = (f32[1,512]{1,0:T(1,128)S(1)}, f32[1,512]{1,0:T(1,128)S(1)}, u32[]{:S(2)}, u32[]{:S(2)}) collective-permute-start(f32[1,512]{1,0:T(1,128)S(1)} %shard_map.129.near_ref), channel_id=1, source_target_pairs={{0,8},{2,10},{4,12},{6,14},{8,0},{10,2},{12,4},{14,6},{1,9},{3,11}... | collective-permute-start | bytes 6152 | tf_op jit(solution)/shard_map/ppermute | solution.py:236
  100.4 4.3 %collective-permute-done.16.across_ref = f32[1,512]{1,0:T(1,128)S(1)} collective-permute-done((f32[1,512]{1,0:T(1,128)S(1)}, f32[1,512]{1,0:T(1,128)S(1)}, u32[]{:S(2)}, u32[]{:S(2)}) %collective-permute-start.16) | collective-permute-done | bytes 2080 | tf_op jit(solution)/shard_map/ppermute | solution.py:236
  105.2 4.8 %collective-permute-start.17 = (bf16[128,640]{1,0:T(8,128)(2,1)S(1)}, bf16[128,640]{1,0:T(8,128)(2,1)S(1)}, u32[]{:S(2)}, u32[]{:S(2)}) collective-permute-start(bf16[128,640]{1,0:T(8,128)(2,1)S(1)} %get-tuple-element.71), channel_id=1, source_target_pairs={{0,1},{1,0},{2,3},{3,2},{4,5},{5,4},{6,7},{7,6},{8,9},{9,8},{10,11... | collective-permute-start | bytes 491528 | tf_op jit(solution)/shard_map/ppermute | solution.py:236
  109.9 3.8 %shard_map.131 = (f32[512,512]{1,0:T(8,128)S(1)}, f32[512,576]{1,0:T(8,128)S(1)}) custom-call(f32[8,512]{1,0:T(8,128)S(1)} %fusion.3.refs_0_, f32[8,512]{1,0:T(8,128)S(1)} %shard_map.115.refs_1_, bf16[512,640]{1,0:T(8,128)(2,1)S(1)} %pad.4.refs_1_.refs_2_, bf16[512,512]{1,0:T(8,128)(2,1)S(1)} %reshape_squeeze.7.refs_2_.refs_3_, ...), custom_call_target="tpu_custom_call" | custom-call | flops 1 | bytes 1 | tf_op jit(solution)/shard_map/pallas_call | solution.py:25
  114.5 15.0 %collective-permute-start.18 = (f32[1,512]{1,0:T(1,128)S(1)}, f32[1,512]{1,0:T(1,128)S(1)}, u32[]{:S(2)}, u32[]{:S(2)}) collective-permute-start(f32[1,512]{1,0:T(1,128)S(1)} %get-tuple-element.82), channel_id=1, source_target_pairs={{0,496},{16,480},{32,464},{48,448},{64,432},{80,416},{96,400},{112... | collective-permute-start | bytes 6152 | tf_op jit(solution)/shard_map/ppermute | solution.py:236
  (67 shorter events, 26.8 us)
Async XLA Ops:
  0.6 24.6 %copy-start.8 = (bf16[1,8,32768]{2,1,0:T(8,128)(2,1)S(1)}, bf16[1,8,32768]{2,1,0:T(8,128)(2,1)}, u32[]{:S(2)}) copy-start(bf16[1,8,32768]{2,1,0:T(8,128)(2,1)} %param.8) | copy-start | bytes 1572868
  9.7 18.2 %collective-permute-start = (bf16[256,640]{1,0:T(8,128)(2,1)S(1)}, bf16[256,640]{1,0:T(8,128)(2,1)S(1)}, u32[]{:S(2)}, u32[]{:S(2)}) collective-permute-start(bf16[256,640]{1,0:T(8,128)(2,1)S(1)} %all_gather.3.refs_3_.refs_4_), channel_id=1, source_target_pairs={{0,2},{2,4},{4,6},{6,8},{8,10},{10,12},{12,14},{14,0},{1,3},{3,5},... | collective-permute-start | bytes 983048 | tf_op jit(solution)/shard_map/ppermute | solution.py:250
  14.8 15.0 %collective-permute-start.2 = (bf16[256,640]{1,0:T(8,128)(2,1)S(1)}, bf16[256,640]{1,0:T(8,128)(2,1)S(1)}, u32[]{:S(2)}, u32[]{:S(2)}) collective-permute-start(bf16[256,640]{1,0:T(8,128)(2,1)S(1)} %all_gather.3.refs_3_.refs_4_), channel_id=1, source_target_pairs={{0,14},{2,0},{4,2},{6,4},{8,6},{10,8},{12,10},{14,12},{1,15},{3,1}... | collective-permute-start | bytes 983048 | tf_op jit(solution)/shard_map/ppermute | solution.py:253
  27.9 10.1 %collective-permute-start.1 = (bf16[256,640]{1,0:T(8,128)(2,1)S(1)}, bf16[256,640]{1,0:T(8,128)(2,1)S(1)}, u32[]{:S(2)}, u32[]{:S(2)}) collective-permute-start(bf16[256,640]{1,0:T(8,128)(2,1)S(1)} %collective-permute-done.refs_3_.refs_4_.refs_5_), channel_id=1, source_target_pairs={{0,2},{2,4},{4,6},{6,8},{8,10},{10,12},{12,14},{14,0},{1,3},{3,5},... | collective-permute-start | bytes 983048 | tf_op jit(solution)/shard_map/ppermute | solution.py:250
  29.8 10.1 %collective-permute-start.4 = (bf16[256,640]{1,0:T(8,128)(2,1)S(1)}, bf16[256,640]{1,0:T(8,128)(2,1)S(1)}, u32[]{:S(2)}, u32[]{:S(2)}) collective-permute-start(bf16[256,640]{1,0:T(8,128)(2,1)S(1)} %collective-permute-done.2.refs_4_.refs_5_.refs_6_), channel_id=1, source_target_pairs={{0,14},{2,0},{4,2},{6,4},{8,6},{10,8},{12,10},{14,12},{1,15},{3,1}... | collective-permute-start | bytes 983048 | tf_op jit(solution)/shard_map/ppermute | solution.py:253
  38.0 9.0 %collective-permute-start.3 = (bf16[256,640]{1,0:T(8,128)(2,1)S(1)}, bf16[256,640]{1,0:T(8,128)(2,1)S(1)}, u32[]{:S(2)}, u32[]{:S(2)}) collective-permute-start(bf16[256,640]{1,0:T(8,128)(2,1)S(1)} %collective-permute-done.1.refs_3_.refs_4_.refs_7_), channel_id=1, source_target_pairs={{0,2},{2,4},{4,6},{6,8},{8,10},{10,12},{12,14},{14,0},{1,3},{3,5},... | collective-permute-start | bytes 983048 | tf_op jit(solution)/shard_map/ppermute | solution.py:250
  39.9 9.0 %collective-permute-start.6 = (bf16[256,640]{1,0:T(8,128)(2,1)S(1)}, bf16[256,640]{1,0:T(8,128)(2,1)S(1)}, u32[]{:S(2)}, u32[]{:S(2)}) collective-permute-start(bf16[256,640]{1,0:T(8,128)(2,1)S(1)} %collective-permute-done.4.refs_4_.refs_5_), channel_id=1, source_target_pairs={{0,14},{2,0},{4,2},{6,4},{8,6},{10,8},{12,10},{14,12},{1,15},{3,1}... | collective-permute-start | bytes 983048 | tf_op jit(solution)/shard_map/ppermute | solution.py:253
  47.0 7.5 %collective-permute-start.5 = (bf16[128,640]{1,0:T(8,128)(2,1)S(1)}, bf16[128,640]{1,0:T(8,128)(2,1)S(1)}, u32[]{:S(2)}, u32[]{:S(2)}) collective-permute-start(bf16[128,640]{1,0:T(8,128)(2,1)S(1)} %slice.6), channel_id=1, source_target_pairs={{0,2},{2,4},{4,6},{6,8},{8,10},{10,12},{12,14},{14,0},{1,3},{3,5},... | collective-permute-start | bytes 491528 | tf_op jit(solution)/shard_map/ppermute | solution.py:250
  49.0 6.8 %collective-permute-start.7 = (bf16[128,640]{1,0:T(8,128)(2,1)S(1)}, bf16[128,640]{1,0:T(8,128)(2,1)S(1)}, u32[]{:S(2)}, u32[]{:S(2)}) collective-permute-start(bf16[128,640]{1,0:T(8,128)(2,1)S(1)} %slice.8), channel_id=1, source_target_pairs={{0,14},{2,0},{4,2},{6,4},{8,6},{10,8},{12,10},{14,12},{1,15},{3,1}... | collective-permute-start | bytes 491528 | tf_op jit(solution)/shard_map/ppermute | solution.py:253
  58.1 8.6 %collective-permute-start.8 = (bf16[128,640]{1,0:T(8,128)(2,1)S(1)}, bf16[128,640]{1,0:T(8,128)(2,1)S(1)}, u32[]{:S(2)}, u32[]{:S(2)}) collective-permute-start(bf16[128,640]{1,0:T(8,128)(2,1)S(1)} %get-tuple-element.53), channel_id=1, source_target_pairs={{0,2},{2,4},{4,6},{6,8},{8,10},{10,12},{12,14},{14,0},{1,3},{3,5},... | collective-permute-start | bytes 491528 | tf_op jit(solution)/shard_map/ppermute | solution.py:250
  60.0 8.7 %collective-permute-start.12 = (bf16[128,640]{1,0:T(8,128)(2,1)S(1)}, bf16[128,640]{1,0:T(8,128)(2,1)S(1)}, u32[]{:S(2)}, u32[]{:S(2)}) collective-permute-start(bf16[128,640]{1,0:T(8,128)(2,1)S(1)} %get-tuple-element.68), channel_id=1, source_target_pairs={{0,14},{2,0},{4,2},{6,4},{8,6},{10,8},{12,10},{14,12},{1,15},{3,1}... | collective-permute-start | bytes 491528 | tf_op jit(solution)/shard_map/ppermute | solution.py:253
  66.7 10.9 %collective-permute-start.9 = (bf16[256,640]{1,0:T(8,128)(2,1)S(1)}, bf16[256,640]{1,0:T(8,128)(2,1)S(1)}, u32[]{:S(2)}, u32[]{:S(2)}) collective-permute-start(bf16[256,640]{1,0:T(8,128)(2,1)S(1)} %shard_map.119), channel_id=1, source_target_pairs={{0,2},{2,4},{4,6},{6,8},{8,10},{10,12},{12,14},{14,0},{1,3},{3,5},... | collective-permute-start | bytes 983048 | tf_op jit(solution)/shard_map/ppermute | solution.py:250
  68.7 11.2 %collective-permute-start.13 = (bf16[256,640]{1,0:T(8,128)(2,1)S(1)}, bf16[256,640]{1,0:T(8,128)(2,1)S(1)}, u32[]{:S(2)}, u32[]{:S(2)}) collective-permute-start(bf16[256,640]{1,0:T(8,128)(2,1)S(1)} %shard_map.126), channel_id=1, source_target_pairs={{0,14},{2,0},{4,2},{6,4},{8,6},{10,8},{12,10},{14,12},{1,15},{3,1}... | collective-permute-start | bytes 983048 | tf_op jit(solution)/shard_map/ppermute | solution.py:253
  77.8 10.4 %collective-permute-start.10 = (bf16[256,640]{1,0:T(8,128)(2,1)S(1)}, bf16[256,640]{1,0:T(8,128)(2,1)S(1)}, u32[]{:S(2)}, u32[]{:S(2)}) collective-permute-start(bf16[256,640]{1,0:T(8,128)(2,1)S(1)} %shard_map.123), channel_id=1, source_target_pairs={{0,2},{2,4},{4,6},{6,8},{8,10},{10,12},{12,14},{14,0},{1,3},{3,5},... | collective-permute-start | bytes 983048 | tf_op jit(solution)/shard_map/ppermute | solution.py:250
  80.1 10.9 %collective-permute-start.14 = (bf16[256,640]{1,0:T(8,128)(2,1)S(1)}, bf16[256,640]{1,0:T(8,128)(2,1)S(1)}, u32[]{:S(2)}, u32[]{:S(2)}) collective-permute-start(bf16[256,640]{1,0:T(8,128)(2,1)S(1)} %shard_map.127), channel_id=1, source_target_pairs={{0,14},{2,0},{4,2},{6,4},{8,6},{10,8},{12,10},{14,12},{1,15},{3,1}... | collective-permute-start | bytes 983048 | tf_op jit(solution)/shard_map/ppermute | solution.py:253
  88.2 16.6 %copy-start.6 = (bf16[256,640]{1,0:T(8,128)(2,1)S(1)}, bf16[256,640]{1,0:T(8,128)(2,1)}, u32[]{:S(2)}) copy-start(bf16[256,640]{1,0:T(8,128)(2,1)} %copy-done.5) | copy-start | bytes 983044
  89.0 15.7 %collective-permute-start.11 = (bf16[256,640]{1,0:T(8,128)(2,1)}, bf16[256,640]{1,0:T(8,128)(2,1)S(1)}, u32[]{:S(2)}, u32[]{:S(2)}) collective-permute-start(bf16[256,640]{1,0:T(8,128)(2,1)} %shard_map.125), channel_id=1, source_target_pairs={{0,2},{2,4},{4,6},{6,8},{8,10},{10,12},{12,14},{14,0},{1,3},{3,5},... | collective-permute-start | bytes 983048 | tf_op jit(solution)/shard_map/ppermute | solution.py:250
  91.8 13.0 %collective-permute-start.15 = (bf16[256,640]{1,0:T(8,128)(2,1)}, bf16[256,640]{1,0:T(8,128)(2,1)S(1)}, u32[]{:S(2)}, u32[]{:S(2)}) collective-permute-start(bf16[256,640]{1,0:T(8,128)(2,1)} %shard_map.128), channel_id=1, source_target_pairs={{0,14},{2,0},{4,2},{6,4},{8,6},{10,8},{12,10},{14,12},{1,15},{3,1}... | collective-permute-start | bytes 983048 | tf_op jit(solution)/shard_map/ppermute | solution.py:253
  96.4 8.3 %collective-permute-start.16 = (f32[1,512]{1,0:T(1,128)S(1)}, f32[1,512]{1,0:T(1,128)S(1)}, u32[]{:S(2)}, u32[]{:S(2)}) collective-permute-start(f32[1,512]{1,0:T(1,128)S(1)} %shard_map.129.near_ref), channel_id=1, source_target_pairs={{0,8},{2,10},{4,12},{6,14},{8,0},{10,2},{12,4},{14,6},{1,9},{3,11}... | collective-permute-start | bytes 6152 | tf_op jit(solution)/shard_map/ppermute | solution.py:236
  105.2 8.5 %copy-start.4 = (bf16[1,128,512]{2,1,0:T(8,128)(2,1)S(1)}, bf16[1,128,512]{2,1,0:T(8,128)(2,1)}, u32[]{:S(2)}) copy-start(bf16[1,128,512]{2,1,0:T(8,128)(2,1)} %param.9) | copy-start | bytes 393220
  105.2 24.4 %copy-start.1 = (f32[512,576]{1,0:T(8,128)S(1)}, f32[512,576]{1,0:T(8,128)}, u32[]{:S(2)}) copy-start(f32[512,576]{1,0:T(8,128)} %copy-done) | copy-start | bytes 3538948
  105.2 8.5 %collective-permute-start.17 = (bf16[128,640]{1,0:T(8,128)(2,1)S(1)}, bf16[128,640]{1,0:T(8,128)(2,1)S(1)}, u32[]{:S(2)}, u32[]{:S(2)}) collective-permute-start(bf16[128,640]{1,0:T(8,128)(2,1)S(1)} %get-tuple-element.71), channel_id=1, source_target_pairs={{0,1},{1,0},{2,3},{3,2},{4,5},{5,4},{6,7},{7,6},{8,9},{9,8},{10,11... | collective-permute-start | bytes 491528 | tf_op jit(solution)/shard_map/ppermute | solution.py:236
  114.5 15.2 %copy-start.3 = (f32[512,512]{1,0:T(8,128)S(1)}, f32[512,512]{1,0:T(8,128)}, u32[]{:S(2)}) copy-start(f32[512,512]{1,0:T(8,128)} %copy-done.2) | copy-start | bytes 3145732
  114.5 18.1 %collective-permute-start.18 = (f32[1,512]{1,0:T(1,128)S(1)}, f32[1,512]{1,0:T(1,128)S(1)}, u32[]{:S(2)}, u32[]{:S(2)}) collective-permute-start(f32[1,512]{1,0:T(1,128)S(1)} %get-tuple-element.82), channel_id=1, source_target_pairs={{0,496},{16,480},{32,464},{48,448},{64,432},{80,416},{96,400},{112... | collective-permute-start | bytes 6152 | tf_op jit(solution)/shard_map/ppermute | solution.py:236
  (4 other events, 21.5 us)

commit v4 on v3

--- a/solution.py
+++ b/solution.py
@@ -91,32 +91,57 @@
     return jnp.where(k_pos <= q_pos, scores, -jnp.inf)
 
 
-def stats_kernel(first, parts, *refs):
-    pos_ref, q_ref, do_ref = refs[:3]
-    k_refs = refs[3 : 3 + parts]
-    out_ref = refs[-1]
-    q_pos = pos_ref[0:1, :]
+def take_stats(q_pos, q_ref, do_ref, k_refs, old):
     scores = [masked_scores(q_pos, q_ref[...], k_ref) for k_ref in k_refs]
     top = fold(jnp.concatenate([fold(s, jnp.maximum) for s in scores]), jnp.maximum)
     top = jnp.max(top, axis=0, keepdims=True)
-    if not first:
-        old = refs[3 + parts]
+    if old is not None:
         top = jnp.maximum(top, old[0:1, :])
-    total, pull = 0.0, 0.0
+    total, pull, kept = 0.0, 0.0, []
     for s, k_ref in zip(scores, k_refs):
         dprob = nt_dot(k_ref[:, :DL], do_ref[...])
         expo = jnp.exp(s - top)
+        kept.append((expo, dprob))
         total = total + fold(expo, jnp.add)
         pull = pull + fold(expo * dprob, jnp.add)
     total = jnp.sum(total, axis=0, keepdims=True)
     pull = jnp.sum(pull, axis=0, keepdims=True)
-    if not first:
+    if old is not None:
         shrink = jnp.exp(old[0:1, :] - top)
         total = total + old[1:2, :] * shrink
         pull = pull + old[2:3, :] * shrink
-    out_ref[0:1, :] = top
-    out_ref[1:2, :] = total
-    out_ref[2:3, :] = pull
+    return top, total, pull, kept
+
+
+def stats_kernel(first, parts, *refs):
+    pos_ref, q_ref, do_ref = refs[:3]
+    old = None if first else refs[3 + parts]
+    out_ref = refs[-1]
+    rows = take_stats(pos_ref[0:1, :], q_ref, do_ref, refs[3 : 3 + parts], old)
+    for i in range(3):
+        out_ref[i : i + 1, :] = rows[i]
+
+
+def last_kernel(pos_ref, q_ref, do_ref, near_ref, far_ref, old_ref, out_ref, *outs):
+    k_refs = (near_ref, far_ref)
+    top, total, pull, kept = take_stats(pos_ref[0:1, :], q_ref, do_ref, k_refs, old_ref)
+    for i, row in enumerate((top, total, pull)):
+        out_ref[i : i + 1, :] = row
+    scale = 1.0 / total
+    delta = pull * scale
+    gain_sum = 0.0
+    for (expo, dprob), k_ref, kg_ref in zip(kept, k_refs, outs):
+        weights = expo * scale
+        dscore = (weights * (dprob - delta) * SCORE_SCALE).astype(BF16)
+        gain_sum = gain_sum + key_grad(weights.astype(BF16), dscore, q_ref, do_ref, k_ref, kg_ref)
+    outs[-1][...] = gain_sum
+
+
+def key_grad(weights, dscore, q_ref, do_ref, k_ref, kg_ref):
+    lat = mm(dscore, q_ref[:, :DL]) + mm(weights, do_ref[...])
+    kg_ref[:, :DL] = lat.astype(BF16)
+    kg_ref[:, DL:] = mm(dscore, q_ref[:, DL:]).astype(BF16)
+    return fold(lat * k_ref[:, :DL].astype(F32), jnp.add)
 
 
 def weights_of(stats_ref, pos_ref, q_ref, k_ref):
@@ -133,20 +158,11 @@
 def key_grad_kernel(parts, *refs):
     pos_ref, stats_ref, q_ref, do_ref = refs[:4]
     k_refs = refs[4 : 4 + parts]
-    kg_refs = refs[4 + parts : -1]
-    split = len(kg_refs) // parts
     gain_sum = 0.0
-    for i, k_ref in enumerate(k_refs):
+    for k_ref, kg_ref in zip(k_refs, refs[4 + parts :]):
         weights = weights_of(stats_ref, pos_ref, q_ref, k_ref)
         dscore = dscore_of(weights, stats_ref, do_ref, k_ref)
-        weights = weights.astype(BF16)
-        lat = mm(dscore, q_ref[:, :DL]) + mm(weights, do_ref[...])
-        rope = mm(dscore, q_ref[:, DL:])
-        for j, kg_ref in enumerate(kg_refs[i * split : (i + 1) * split]):
-            at = slice(j * kg_ref.shape[0], (j + 1) * kg_ref.shape[0])
-            kg_ref[:, :DL] = lat[at].astype(BF16)
-            kg_ref[:, DL:] = rope[at].astype(BF16)
-        gain_sum = gain_sum + fold(lat * k_ref[:, :DL].astype(F32), jnp.add)
+        gain_sum = gain_sum + key_grad(weights.astype(BF16), dscore, q_ref, do_ref, k_ref, kg_ref)
     refs[-1][...] = gain_sum
 
 
@@ -215,7 +231,15 @@
     far_ref[0:16, QKW:] = spread(total)
 
 
-def latent_kernel(section_ref, own_ref, far_ref, latent_ref, gain_ref, sum_ref, lg_ref, rg_ref, gg_ref):
+def sum_kernel(sum_ref, far_ref, out_ref):
+    out_ref[...] = sum_ref[...] + gathered(far_ref)
+
+
+def plus_kernel(one_ref, two_ref, out_ref):
+    out_ref[...] = one_ref[...] + two_ref[...]
+
+
+def latent_kernel(section_ref, own_ref, far_ref, latent_ref, gain_ref, lg_ref, rg_ref):
     gain = section_gain(gain_ref, section_ref)
     latent = latent_ref[...].astype(F32)
     inverse = lax.rsqrt(jnp.mean(latent * latent, axis=-1, keepdims=True) + 1e-06)
@@ -224,7 +248,6 @@
     mean = jnp.mean(gated * latent, axis=-1, keepdims=True)
     lg_ref[...] = (inverse * gated - latent * (inverse * inverse * inverse) * mean).astype(BF16)
     rg_ref[...] = total[:, DL:QKW].T.astype(BF16)
-    gg_ref[...] = sum_ref[...] + gathered(far_ref)
 
 
 def after(value, *first):
@@ -272,7 +295,7 @@
     token = jnp.arange(8 * rows, dtype=jnp.int32).reshape(8, rows) % rows // HEADS
     q_pos = (query_start[0, 0] + token).astype(F32)
 
-    def take_stats(held, stats):
+    def add_stats(held, stats):
         args = [q_pos, q, do, *held] + ([] if stats is None else [stats])
         return call(
             lambda *refs: stats_kernel(stats is None, len(held), *refs),
@@ -281,12 +304,11 @@
             args,
         )
 
-    def key_grads(held, split=1):
+    def key_grads(held):
         args = [q_pos, stats, q, do, *held]
-        sizes = [piece.shape[0] // split for piece in held for _ in range(split)]
         return call(
             lambda *refs: key_grad_kernel(len(held), *refs),
-            [shape(size, WIDE, BF16) for size in sizes] + [shape(8, DL, F32)],
+            [shape(piece.shape[0], WIDE, BF16) for piece in held] + [shape(8, DL, F32)],
             [VMEM] * len(args),
             args,
         )
@@ -308,17 +330,22 @@
     r1, l1 = right(pair), left(pair)
     r1, q, do = after(r1, q, do)
     r2, l2 = right(r1), left(l1)
-    stats = take_stats([pair], None)
-    stats = take_stats([r1, l1], stats)
+    stats = add_stats([pair], None)
+    stats = add_stats([r1, l1], stats)
     r2, stats = after(r2, stats)
     r3, l3 = right(r2), left(l2)
-    stats = take_stats([r2, l2], stats)
+    stats = add_stats([r2, l2], stats)
     r3, stats = after(r3, stats)
     r4, l4 = right(r3[:own]), left(l3[own:])
-    stats = take_stats([r3, l3], stats)
-    stats = take_stats([r4, l4], stats)
-
-    kr4, kl4, g4 = key_grads([r4, l4])
+    stats = add_stats([r3, l3], stats)
+
+    args = (q_pos, q, do, r4, l4, stats)
+    stats, kr4, kl4, g4 = call(
+        last_kernel,
+        [shape(8, rows, F32), shape(own, WIDE, BF16), shape(own, WIDE, BF16), shape(8, DL, F32)],
+        [VMEM] * len(args),
+        args,
+    )
     ahead, behind = right(kr4), left(kl4)
     kr3, kl3, g3 = key_grads([r3, l3])
     ahead, behind = right(add(kl3, ahead, half=0)), left(add(kr3, behind, half=1))
@@ -347,13 +374,16 @@
     other = swap(other, "x", 1)
     second = query_side([l2, r3, l3, r4, l4])
     other, *second = after(other, *second)
-    latent_grad, rope_grad, gain_sum = call(
+    gain_sum = call(sum_kernel, shape(1, DL, F32), [VMEM] * 2, (gain_sum, other))
+    mirror = swap(gain_sum, "pipe", n_pipe - 1)
+    other, gain_sum = after(other, gain_sum)
+    latent_grad, rope_grad = call(
         latent_kernel,
-        [shape(own, DL, BF16), shape(DR, own, BF16), shape(1, DL, F32)],
-        [SMEM] + [VMEM] * 5,
-        (section, mine, other, latent[0], gain, gain_sum),
-    )
-    gain_sum = gain_sum + swap(gain_sum, "pipe", n_pipe - 1)
+        [shape(own, DL, BF16), shape(DR, own, BF16)],
+        [SMEM] + [VMEM] * 4,
+        (section, mine, other, latent[0], gain),
+    )
+    gain_sum = call(plus_kernel, shape(1, DL, F32), [VMEM] * 2, (gain_sum, mirror))
     return (
         *((a + b).astype(BF16).reshape(1, tokens, -1) for a, b in zip(first, second)),
         latent_grad[None],

time: 134 us -> 134 us (level)
    pallas_call x23 -> x24, Pallas kernels: 23.9 us -> 23.7 us  [call(): pl.pallas_call(kernel, out_shape=out, in_specs=ins, out_specs=jax.tree.ma...]
  transfers between devices with their start and end apart: 19 -> 19, of which waited for: 5 -> 5; matrix products, arithmetic and copies ran while one was open for 4% -> 4% of each run, Pallas kernels for 14% -> 15%
where the time goes in v4:
time: 134 us; the launch traced here: 133 us
  starting transfers between devices  83.5 us (62%)
  Pallas kernels  23.7 us (18%)
  waiting for transfers between devices  11 us (8%)
  blocking collectives  7.21 us (5%)
  local copies, waits for them, and re-layouts  5.52 us (4%)
  between operations  1.79 us (1%)
    ppermute x8, starting transfers between devices, left(): return lax.ppermute(value, 'z', [(i, (i - 1) % n_z) for i in range(n_z)])  41.2 us
    ppermute x3, starting transfers between devices, swap(): return lax.ppermute(value, axis, [(i, i ^ mask) for i in range(size)])  23.8 us
    pallas_call x24, Pallas kernels, call(): pl.pallas_call(kernel, out_shape=out, in_specs=ins, out_specs=jax.tree.ma...  23.7 us
    ppermute x8, starting transfers between devices, right(): return lax.ppermute(value, 'z', [(i, (i + 1) % n_z) for i in range(n_z)])  18.5 us
    all_gather x1, blocking collectives, shards(): pair = lax.all_gather(local, 'x', axis=0, tiled=True)  7.21 us
    ppermute x8, waiting for transfers between devices, right(): return lax.ppermute(value, 'z', [(i, (i + 1) % n_z) for i in range(n_z)])  5.34 us
    ppermute x3, waiting for transfers between devices, swap(): return lax.ppermute(value, axis, [(i, i ^ mask) for i in range(size)])  4.34 us
  transfers between devices with their start and end apart: 19, of which 5 were waited for; matrix products, arithmetic and copies ran while one was open for 4% of the time, Pallas kernels for 15%

profile of v4, /device:TPU:1, one launch (start us, length us, event | category | flops | bytes accessed | tf_op | source)
XLA Modules:
  0.0 133.2 jit_solution(14584749786937706642)
XLA Ops:
  2.5 7.2 %all_gather.3.refs_3_.refs_4_ = bf16[256,640]{1,0:T(8,128)(2,1)S(1)} all-gather(bf16[128,640]{1,0:T(8,128)(2,1)} %shard_map.110), channel_id=1, replica_groups=mesh['pipe'=32,'z'=8,'x'=2] {'x'}, dimensions={0}, use_global_device_ids=true | all-gather | bytes 491520 | tf_op jit(solution)/shard_map/all_gather | solution.py:292
  9.7 5.1 %collective-permute-start = (bf16[256,640]{1,0:T(8,128)(2,1)S(1)}, bf16[256,640]{1,0:T(8,128)(2,1)S(1)}, u32[]{:S(2)}, u32[]{:S(2)}) collective-permute-start(bf16[256,640]{1,0:T(8,128)(2,1)S(1)} %all_gather.3.refs_3_.refs_4_), channel_id=1, source_target_pairs={{0,2},{2,4},{4,6},{6,8},{8,10},{10,12},{12,14},{14,0},{1,3},{3,5},... | collective-permute-start | bytes 983048 | tf_op jit(solution)/shard_map/ppermute | solution.py:273
  14.8 8.6 %collective-permute-start.2 = (bf16[256,640]{1,0:T(8,128)(2,1)S(1)}, bf16[256,640]{1,0:T(8,128)(2,1)S(1)}, u32[]{:S(2)}, u32[]{:S(2)}) collective-permute-start(bf16[256,640]{1,0:T(8,128)(2,1)S(1)} %all_gather.3.refs_3_.refs_4_), channel_id=1, source_target_pairs={{0,14},{2,0},{4,2},{6,4},{8,6},{10,8},{12,10},{14,12},{1,15},{3,1}... | collective-permute-start | bytes 983048 | tf_op jit(solution)/shard_map/ppermute | solution.py:276
  25.5 2.3 %collective-permute-done.refs_3_.refs_4_.refs_5_ = bf16[256,640]{1,0:T(8,128)(2,1)S(1)} collective-permute-done((bf16[256,640]{1,0:T(8,128)(2,1)S(1)}, bf16[256,640]{1,0:T(8,128)(2,1)S(1)}, u32[]{:S(2)}, u32[]{:S(2)}) %collective-permute-start) | collective-permute-done | bytes 327712 | tf_op jit(solution)/shard_map/ppermute | solution.py:273
  27.9 1.9 %collective-permute-start.1 = (bf16[256,640]{1,0:T(8,128)(2,1)S(1)}, bf16[256,640]{1,0:T(8,128)(2,1)S(1)}, u32[]{:S(2)}, u32[]{:S(2)}) collective-permute-start(bf16[256,640]{1,0:T(8,128)(2,1)S(1)} %collective-permute-done.refs_3_.refs_4_.refs_5_), channel_id=1, source_target_pairs={{0,2},{2,4},{4,6},{6,8},{8,10},{10,12},{12,14},{14,0},{1,3},{3,5},... | collective-permute-start | bytes 983048 | tf_op jit(solution)/shard_map/ppermute | solution.py:273
  29.8 4.6 %collective-permute-start.4 = (bf16[256,640]{1,0:T(8,128)(2,1)S(1)}, bf16[256,640]{1,0:T(8,128)(2,1)S(1)}, u32[]{:S(2)}, u32[]{:S(2)}) collective-permute-start(bf16[256,640]{1,0:T(8,128)(2,1)S(1)} %collective-permute-done.2.refs_4_.refs_5_.refs_6_), channel_id=1, source_target_pairs={{0,14},{2,0},{4,2},{6,4},{8,6},{10,8},{12,10},{14,12},{1,15},{3,1}... | collective-permute-start | bytes 983048 | tf_op jit(solution)/shard_map/ppermute | solution.py:276
  38.0 1.9 %collective-permute-start.3 = (bf16[256,640]{1,0:T(8,128)(2,1)S(1)}, bf16[256,640]{1,0:T(8,128)(2,1)S(1)}, u32[]{:S(2)}, u32[]{:S(2)}) collective-permute-start(bf16[256,640]{1,0:T(8,128)(2,1)S(1)} %collective-permute-done.1.refs_3_.refs_4_.refs_7_), channel_id=1, source_target_pairs={{0,2},{2,4},{4,6},{6,8},{8,10},{10,12},{12,14},{14,0},{1,3},{3,5},... | collective-permute-start | bytes 983048 | tf_op jit(solution)/shard_map/ppermute | solution.py:273
  39.9 4.6 %collective-permute-start.6 = (bf16[256,640]{1,0:T(8,128)(2,1)S(1)}, bf16[256,640]{1,0:T(8,128)(2,1)S(1)}, u32[]{:S(2)}, u32[]{:S(2)}) collective-permute-start(bf16[256,640]{1,0:T(8,128)(2,1)S(1)} %collective-permute-done.4.refs_4_.refs_5_), channel_id=1, source_target_pairs={{0,14},{2,0},{4,2},{6,4},{8,6},{10,8},{12,10},{14,12},{1,15},{3,1}... | collective-permute-start | bytes 983048 | tf_op jit(solution)/shard_map/ppermute | solution.py:276
  47.0 1.9 %collective-permute-start.5 = (bf16[128,640]{1,0:T(8,128)(2,1)S(1)}, bf16[128,640]{1,0:T(8,128)(2,1)S(1)}, u32[]{:S(2)}, u32[]{:S(2)}) collective-permute-start(bf16[128,640]{1,0:T(8,128)(2,1)S(1)} %slice.6), channel_id=1, source_target_pairs={{0,2},{2,4},{4,6},{6,8},{8,10},{10,12},{12,14},{14,0},{1,3},{3,5},... | collective-permute-start | bytes 491528 | tf_op jit(solution)/shard_map/ppermute | solution.py:273
  49.0 4.6 %collective-permute-start.7 = (bf16[128,640]{1,0:T(8,128)(2,1)S(1)}, bf16[128,640]{1,0:T(8,128)(2,1)S(1)}, u32[]{:S(2)}, u32[]{:S(2)}) collective-permute-start(bf16[128,640]{1,0:T(8,128)(2,1)S(1)} %slice.8), channel_id=1, source_target_pairs={{0,14},{2,0},{4,2},{6,4},{8,6},{10,8},{12,10},{14,12},{1,15},{3,1}... | collective-permute-start | bytes 491528 | tf_op jit(solution)/shard_map/ppermute | solution.py:276
  57.3 1.9 %collective-permute-start.8 = (bf16[128,640]{1,0:T(8,128)(2,1)S(1)}, bf16[128,640]{1,0:T(8,128)(2,1)S(1)}, u32[]{:S(2)}, u32[]{:S(2)}) collective-permute-start(bf16[128,640]{1,0:T(8,128)(2,1)S(1)} %get-tuple-element.56), channel_id=1, source_target_pairs={{0,2},{2,4},{4,6},{6,8},{8,10},{10,12},{12,14},{14,0},{1,3},{3,5},... | collective-permute-start | bytes 491528 | tf_op jit(solution)/shard_map/ppermute | solution.py:273
  59.2 5.0 %collective-permute-start.12 = (bf16[128,640]{1,0:T(8,128)(2,1)S(1)}, bf16[128,640]{1,0:T(8,128)(2,1)S(1)}, u32[]{:S(2)}, u32[]{:S(2)}) collective-permute-start(bf16[128,640]{1,0:T(8,128)(2,1)S(1)} %get-tuple-element.71), channel_id=1, source_target_pairs={{0,14},{2,0},{4,2},{6,4},{8,6},{10,8},{12,10},{14,12},{1,15},{3,1}... | collective-permute-start | bytes 491528 | tf_op jit(solution)/shard_map/ppermute | solution.py:276
  66.0 1.9 %collective-permute-start.9 = (bf16[256,640]{1,0:T(8,128)(2,1)S(1)}, bf16[256,640]{1,0:T(8,128)(2,1)S(1)}, u32[]{:S(2)}, u32[]{:S(2)}) collective-permute-start(bf16[256,640]{1,0:T(8,128)(2,1)S(1)} %shard_map.118), channel_id=1, source_target_pairs={{0,2},{2,4},{4,6},{6,8},{8,10},{10,12},{12,14},{14,0},{1,3},{3,5},... | collective-permute-start | bytes 983048 | tf_op jit(solution)/shard_map/ppermute | solution.py:273
  67.9 4.6 %collective-permute-start.13 = (bf16[256,640]{1,0:T(8,128)(2,1)S(1)}, bf16[256,640]{1,0:T(8,128)(2,1)S(1)}, u32[]{:S(2)}, u32[]{:S(2)}) collective-permute-start(bf16[256,640]{1,0:T(8,128)(2,1)S(1)} %shard_map.125), channel_id=1, source_target_pairs={{0,14},{2,0},{4,2},{6,4},{8,6},{10,8},{12,10},{14,12},{1,15},{3,1}... | collective-permute-start | bytes 983048 | tf_op jit(solution)/shard_map/ppermute | solution.py:276
  77.0 1.9 %collective-permute-start.10 = (bf16[256,640]{1,0:T(8,128)(2,1)S(1)}, bf16[256,640]{1,0:T(8,128)(2,1)S(1)}, u32[]{:S(2)}, u32[]{:S(2)}) collective-permute-start(bf16[256,640]{1,0:T(8,128)(2,1)S(1)} %shard_map.122), channel_id=1, source_target_pairs={{0,2},{2,4},{4,6},{6,8},{8,10},{10,12},{12,14},{14,0},{1,3},{3,5},... | collective-permute-start | bytes 983048 | tf_op jit(solution)/shard_map/ppermute | solution.py:273
  79.1 4.8 %collective-permute-start.14 = (bf16[256,640]{1,0:T(8,128)(2,1)S(1)}, bf16[256,640]{1,0:T(8,128)(2,1)S(1)}, u32[]{:S(2)}, u32[]{:S(2)}) collective-permute-start(bf16[256,640]{1,0:T(8,128)(2,1)S(1)} %shard_map.126), channel_id=1, source_target_pairs={{0,14},{2,0},{4,2},{6,4},{8,6},{10,8},{12,10},{14,12},{1,15},{3,1}... | collective-permute-start | bytes 983048 | tf_op jit(solution)/shard_map/ppermute | solution.py:276
  83.8 3.5 %shard_map.123 = (f32[512,512]{1,0:T(8,128)S(1)}, f32[512,576]{1,0:T(8,128)S(1)}) custom-call(f32[8,512]{1,0:T(8,128)S(1)} %fusion.3.refs_0_.pos_ref, f32[8,512]{1,0:T(8,128)S(1)} %get-tuple-element.53.refs_1_, bf16[512,640]{1,0:T(8,128)(2,1)S(1)} %pad.4.refs_1_.q_ref.refs_2_, bf16[512,512]{1,0:T(8,128)(2,1)S(1)} %reshape_squeeze.7.refs_2_.do_ref.refs_3_, ...), custom_call_target="tpu_custom_call" | custom-call | flops 1 | bytes 1 | tf_op jit(solution)/shard_map/pallas_call | solution.py:25
  88.2 1.9 %collective-permute-start.11 = (bf16[256,640]{1,0:T(8,128)(2,1)}, bf16[256,640]{1,0:T(8,128)(2,1)S(1)}, u32[]{:S(2)}, u32[]{:S(2)}) collective-permute-start(bf16[256,640]{1,0:T(8,128)(2,1)} %shard_map.124), channel_id=1, source_target_pairs={{0,2},{2,4},{4,6},{6,8},{8,10},{10,12},{12,14},{14,0},{1,3},{3,5},... | collective-permute-start | bytes 983048 | tf_op jit(solution)/shard_map/ppermute | solution.py:273
  90.9 4.6 %collective-permute-start.15 = (bf16[256,640]{1,0:T(8,128)(2,1)}, bf16[256,640]{1,0:T(8,128)(2,1)S(1)}, u32[]{:S(2)}, u32[]{:S(2)}) collective-permute-start(bf16[256,640]{1,0:T(8,128)(2,1)} %shard_map.127), channel_id=1, source_target_pairs={{0,14},{2,0},{4,2},{6,4},{8,6},{10,8},{12,10},{14,12},{1,15},{3,1}... | collective-permute-start | bytes 983048 | tf_op jit(solution)/shard_map/ppermute | solution.py:276
  95.6 4.0 %collective-permute-start.16 = (f32[1,512]{1,0:T(1,128)S(1)}, f32[1,512]{1,0:T(1,128)S(1)}, u32[]{:S(2)}, u32[]{:S(2)}) collective-permute-start(f32[1,512]{1,0:T(1,128)S(1)} %shard_map.128.near_ref), channel_id=1, source_target_pairs={{0,8},{2,10},{4,12},{6,14},{8,0},{10,2},{12,4},{14,6},{1,9},{3,11}... | collective-permute-start | bytes 6152 | tf_op jit(solution)/shard_map/ppermute | solution.py:259
  99.6 4.3 %collective-permute-done.16.across_ref = f32[1,512]{1,0:T(1,128)S(1)} collective-permute-done((f32[1,512]{1,0:T(1,128)S(1)}, f32[1,512]{1,0:T(1,128)S(1)}, u32[]{:S(2)}, u32[]{:S(2)}) %collective-permute-start.16) | collective-permute-done | bytes 2080 | tf_op jit(solution)/shard_map/ppermute | solution.py:259
  104.3 4.8 %collective-permute-start.17 = (bf16[128,640]{1,0:T(8,128)(2,1)S(1)}, bf16[128,640]{1,0:T(8,128)(2,1)S(1)}, u32[]{:S(2)}, u32[]{:S(2)}) collective-permute-start(bf16[128,640]{1,0:T(8,128)(2,1)S(1)} %get-tuple-element.74), channel_id=1, source_target_pairs={{0,1},{1,0},{2,3},{3,2},{4,5},{5,4},{6,7},{7,6},{8,9},{9,8},{10,11... | collective-permute-start | bytes 491528 | tf_op jit(solution)/shard_map/ppermute | solution.py:259
  109.1 3.8 %shard_map.130 = (f32[512,512]{1,0:T(8,128)S(1)}, f32[512,576]{1,0:T(8,128)S(1)}) custom-call(f32[8,512]{1,0:T(8,128)S(1)} %fusion.3.refs_0_.pos_ref, f32[8,512]{1,0:T(8,128)S(1)} %get-tuple-element.53.refs_1_, bf16[512,640]{1,0:T(8,128)(2,1)S(1)} %pad.4.refs_1_.q_ref.refs_2_, bf16[512,512]{1,0:T(8,128)(2,1)S(1)} %reshape_squeeze.7.refs_2_.do_ref.refs_3_, ...), custom_call_target="tpu_custom_call" | custom-call | flops 1 | bytes 1 | tf_op jit(solution)/shard_map/pallas_call | solution.py:25
  113.0 15.0 %collective-permute-start.18 = (f32[1,512]{1,0:T(1,128)S(1)}, f32[1,512]{1,0:T(1,128)S(1)}, u32[]{:S(2)}, u32[]{:S(2)}) collective-permute-start(f32[1,512]{1,0:T(1,128)S(1)} %shard_map.131.one_ref), channel_id=1, source_target_pairs={{0,496},{16,480},{32,464},{48,448},{64,432},{80,416},{96,400},{112... | collective-permute-start | bytes 6152 | tf_op jit(solution)/shard_map/ppermute | solution.py:259
  (67 shorter events, 26.8 us)
Async XLA Ops:
  0.6 24.6 %copy-start.8 = (bf16[1,8,32768]{2,1,0:T(8,128)(2,1)S(1)}, bf16[1,8,32768]{2,1,0:T(8,128)(2,1)}, u32[]{:S(2)}) copy-start(bf16[1,8,32768]{2,1,0:T(8,128)(2,1)} %param.8) | copy-start | bytes 1572868
  9.7 18.2 %collective-permute-start = (bf16[256,640]{1,0:T(8,128)(2,1)S(1)}, bf16[256,640]{1,0:T(8,128)(2,1)S(1)}, u32[]{:S(2)}, u32[]{:S(2)}) collective-permute-start(bf16[256,640]{1,0:T(8,128)(2,1)S(1)} %all_gather.3.refs_3_.refs_4_), channel_id=1, source_target_pairs={{0,2},{2,4},{4,6},{6,8},{8,10},{10,12},{12,14},{14,0},{1,3},{3,5},... | collective-permute-start | bytes 983048 | tf_op jit(solution)/shard_map/ppermute | solution.py:273
  14.8 15.0 %collective-permute-start.2 = (bf16[256,640]{1,0:T(8,128)(2,1)S(1)}, bf16[256,640]{1,0:T(8,128)(2,1)S(1)}, u32[]{:S(2)}, u32[]{:S(2)}) collective-permute-start(bf16[256,640]{1,0:T(8,128)(2,1)S(1)} %all_gather.3.refs_3_.refs_4_), channel_id=1, source_target_pairs={{0,14},{2,0},{4,2},{6,4},{8,6},{10,8},{12,10},{14,12},{1,15},{3,1}... | collective-permute-start | bytes 983048 | tf_op jit(solution)/shard_map/ppermute | solution.py:276
  27.9 10.1 %collective-permute-start.1 = (bf16[256,640]{1,0:T(8,128)(2,1)S(1)}, bf16[256,640]{1,0:T(8,128)(2,1)S(1)}, u32[]{:S(2)}, u32[]{:S(2)}) collective-permute-start(bf16[256,640]{1,0:T(8,128)(2,1)S(1)} %collective-permute-done.refs_3_.refs_4_.refs_5_), channel_id=1, source_target_pairs={{0,2},{2,4},{4,6},{6,8},{8,10},{10,12},{12,14},{14,0},{1,3},{3,5},... | collective-permute-start | bytes 983048 | tf_op jit(solution)/shard_map/ppermute | solution.py:273
  29.8 10.1 %collective-permute-start.4 = (bf16[256,640]{1,0:T(8,128)(2,1)S(1)}, bf16[256,640]{1,0:T(8,128)(2,1)S(1)}, u32[]{:S(2)}, u32[]{:S(2)}) collective-permute-start(bf16[256,640]{1,0:T(8,128)(2,1)S(1)} %collective-permute-done.2.refs_4_.refs_5_.refs_6_), channel_id=1, source_target_pairs={{0,14},{2,0},{4,2},{6,4},{8,6},{10,8},{12,10},{14,12},{1,15},{3,1}... | collective-permute-start | bytes 983048 | tf_op jit(solution)/shard_map/ppermute | solution.py:276
  38.0 9.0 %collective-permute-start.3 = (bf16[256,640]{1,0:T(8,128)(2,1)S(1)}, bf16[256,640]{1,0:T(8,128)(2,1)S(1)}, u32[]{:S(2)}, u32[]{:S(2)}) collective-permute-start(bf16[256,640]{1,0:T(8,128)(2,1)S(1)} %collective-permute-done.1.refs_3_.refs_4_.refs_7_), channel_id=1, source_target_pairs={{0,2},{2,4},{4,6},{6,8},{8,10},{10,12},{12,14},{14,0},{1,3},{3,5},... | collective-permute-start | bytes 983048 | tf_op jit(solution)/shard_map/ppermute | solution.py:273
  39.9 9.0 %collective-permute-start.6 = (bf16[256,640]{1,0:T(8,128)(2,1)S(1)}, bf16[256,640]{1,0:T(8,128)(2,1)S(1)}, u32[]{:S(2)}, u32[]{:S(2)}) collective-permute-start(bf16[256,640]{1,0:T(8,128)(2,1)S(1)} %collective-permute-done.4.refs_4_.refs_5_), channel_id=1, source_target_pairs={{0,14},{2,0},{4,2},{6,4},{8,6},{10,8},{12,10},{14,12},{1,15},{3,1}... | collective-permute-start | bytes 983048 | tf_op jit(solution)/shard_map/ppermute | solution.py:276
  47.0 7.5 %collective-permute-start.5 = (bf16[128,640]{1,0:T(8,128)(2,1)S(1)}, bf16[128,640]{1,0:T(8,128)(2,1)S(1)}, u32[]{:S(2)}, u32[]{:S(2)}) collective-permute-start(bf16[128,640]{1,0:T(8,128)(2,1)S(1)} %slice.6), channel_id=1, source_target_pairs={{0,2},{2,4},{4,6},{6,8},{8,10},{10,12},{12,14},{14,0},{1,3},{3,5},... | collective-permute-start | bytes 491528 | tf_op jit(solution)/shard_map/ppermute | solution.py:273
  49.0 6.8 %collective-permute-start.7 = (bf16[128,640]{1,0:T(8,128)(2,1)S(1)}, bf16[128,640]{1,0:T(8,128)(2,1)S(1)}, u32[]{:S(2)}, u32[]{:S(2)}) collective-permute-start(bf16[128,640]{1,0:T(8,128)(2,1)S(1)} %slice.8), channel_id=1, source_target_pairs={{0,14},{2,0},{4,2},{6,4},{8,6},{10,8},{12,10},{14,12},{1,15},{3,1}... | collective-permute-start | bytes 491528 | tf_op jit(solution)/shard_map/ppermute | solution.py:276
  57.3 8.6 %collective-permute-start.8 = (bf16[128,640]{1,0:T(8,128)(2,1)S(1)}, bf16[128,640]{1,0:T(8,128)(2,1)S(1)}, u32[]{:S(2)}, u32[]{:S(2)}) collective-permute-start(bf16[128,640]{1,0:T(8,128)(2,1)S(1)} %get-tuple-element.56), channel_id=1, source_target_pairs={{0,2},{2,4},{4,6},{6,8},{8,10},{10,12},{12,14},{14,0},{1,3},{3,5},... | collective-permute-start | bytes 491528 | tf_op jit(solution)/shard_map/ppermute | solution.py:273
  59.2 8.7 %collective-permute-start.12 = (bf16[128,640]{1,0:T(8,128)(2,1)S(1)}, bf16[128,640]{1,0:T(8,128)(2,1)S(1)}, u32[]{:S(2)}, u32[]{:S(2)}) collective-permute-start(bf16[128,640]{1,0:T(8,128)(2,1)S(1)} %get-tuple-element.71), channel_id=1, source_target_pairs={{0,14},{2,0},{4,2},{6,4},{8,6},{10,8},{12,10},{14,12},{1,15},{3,1}... | collective-permute-start | bytes 491528 | tf_op jit(solution)/shard_map/ppermute | solution.py:276
  66.0 10.9 %collective-permute-start.9 = (bf16[256,640]{1,0:T(8,128)(2,1)S(1)}, bf16[256,640]{1,0:T(8,128)(2,1)S(1)}, u32[]{:S(2)}, u32[]{:S(2)}) collective-permute-start(bf16[256,640]{1,0:T(8,128)(2,1)S(1)} %shard_map.118), channel_id=1, source_target_pairs={{0,2},{2,4},{4,6},{6,8},{8,10},{10,12},{12,14},{14,0},{1,3},{3,5},... | collective-permute-start | bytes 983048 | tf_op jit(solution)/shard_map/ppermute | solution.py:273
  67.9 11.0 %collective-permute-start.13 = (bf16[256,640]{1,0:T(8,128)(2,1)S(1)}, bf16[256,640]{1,0:T(8,128)(2,1)S(1)}, u32[]{:S(2)}, u32[]{:S(2)}) collective-permute-start(bf16[256,640]{1,0:T(8,128)(2,1)S(1)} %shard_map.125), channel_id=1, source_target_pairs={{0,14},{2,0},{4,2},{6,4},{8,6},{10,8},{12,10},{14,12},{1,15},{3,1}... | collective-permute-start | bytes 983048 | tf_op jit(solution)/shard_map/ppermute | solution.py:276
  77.0 10.4 %collective-permute-start.10 = (bf16[256,640]{1,0:T(8,128)(2,1)S(1)}, bf16[256,640]{1,0:T(8,128)(2,1)S(1)}, u32[]{:S(2)}, u32[]{:S(2)}) collective-permute-start(bf16[256,640]{1,0:T(8,128)(2,1)S(1)} %shard_map.122), channel_id=1, source_target_pairs={{0,2},{2,4},{4,6},{6,8},{8,10},{10,12},{12,14},{14,0},{1,3},{3,5},... | collective-permute-start | bytes 983048 | tf_op jit(solution)/shard_map/ppermute | solution.py:273
  79.1 11.0 %collective-permute-start.14 = (bf16[256,640]{1,0:T(8,128)(2,1)S(1)}, bf16[256,640]{1,0:T(8,128)(2,1)S(1)}, u32[]{:S(2)}, u32[]{:S(2)}) collective-permute-start(bf16[256,640]{1,0:T(8,128)(2,1)S(1)} %shard_map.126), channel_id=1, source_target_pairs={{0,14},{2,0},{4,2},{6,4},{8,6},{10,8},{12,10},{14,12},{1,15},{3,1}... | collective-permute-start | bytes 983048 | tf_op jit(solution)/shard_map/ppermute | solution.py:276
  87.3 8.2 %copy-start = (f32[512,576]{1,0:T(8,128)}, f32[512,576]{1,0:T(8,128)S(1)}, u32[]{:S(2)}) copy-start(f32[512,576]{1,0:T(8,128)S(1)} %get-tuple-element.78) | copy-start | bytes 3538948
  87.4 16.6 %copy-start.6 = (bf16[256,640]{1,0:T(8,128)(2,1)S(1)}, bf16[256,640]{1,0:T(8,128)(2,1)}, u32[]{:S(2)}) copy-start(bf16[256,640]{1,0:T(8,128)(2,1)} %copy-done.5) | copy-start | bytes 983044
  88.2 15.7 %collective-permute-start.11 = (bf16[256,640]{1,0:T(8,128)(2,1)}, bf16[256,640]{1,0:T(8,128)(2,1)S(1)}, u32[]{:S(2)}, u32[]{:S(2)}) collective-permute-start(bf16[256,640]{1,0:T(8,128)(2,1)} %shard_map.124), channel_id=1, source_target_pairs={{0,2},{2,4},{4,6},{6,8},{8,10},{10,12},{12,14},{14,0},{1,3},{3,5},... | collective-permute-start | bytes 983048 | tf_op jit(solution)/shard_map/ppermute | solution.py:273
  90.9 13.0 %collective-permute-start.15 = (bf16[256,640]{1,0:T(8,128)(2,1)}, bf16[256,640]{1,0:T(8,128)(2,1)S(1)}, u32[]{:S(2)}, u32[]{:S(2)}) collective-permute-start(bf16[256,640]{1,0:T(8,128)(2,1)} %shard_map.127), channel_id=1, source_target_pairs={{0,14},{2,0},{4,2},{6,4},{8,6},{10,8},{12,10},{14,12},{1,15},{3,1}... | collective-permute-start | bytes 983048 | tf_op jit(solution)/shard_map/ppermute | solution.py:276
  95.6 8.3 %collective-permute-start.16 = (f32[1,512]{1,0:T(1,128)S(1)}, f32[1,512]{1,0:T(1,128)S(1)}, u32[]{:S(2)}, u32[]{:S(2)}) collective-permute-start(f32[1,512]{1,0:T(1,128)S(1)} %shard_map.128.near_ref), channel_id=1, source_target_pairs={{0,8},{2,10},{4,12},{6,14},{8,0},{10,2},{12,4},{14,6},{1,9},{3,11}... | collective-permute-start | bytes 6152 | tf_op jit(solution)/shard_map/ppermute | solution.py:259
  104.3 23.7 %copy-start.1 = (f32[512,576]{1,0:T(8,128)S(1)}, f32[512,576]{1,0:T(8,128)}, u32[]{:S(2)}) copy-start(f32[512,576]{1,0:T(8,128)} %copy-done) | copy-start | bytes 3538948
  104.3 8.6 %collective-permute-start.17 = (bf16[128,640]{1,0:T(8,128)(2,1)S(1)}, bf16[128,640]{1,0:T(8,128)(2,1)S(1)}, u32[]{:S(2)}, u32[]{:S(2)}) collective-permute-start(bf16[128,640]{1,0:T(8,128)(2,1)S(1)} %get-tuple-element.74), channel_id=1, source_target_pairs={{0,1},{1,0},{2,3},{3,2},{4,5},{5,4},{6,7},{7,6},{8,9},{9,8},{10,11... | collective-permute-start | bytes 491528 | tf_op jit(solution)/shard_map/ppermute | solution.py:259
  113.0 15.3 %copy-start.3 = (f32[512,512]{1,0:T(8,128)S(1)}, f32[512,512]{1,0:T(8,128)}, u32[]{:S(2)}) copy-start(f32[512,512]{1,0:T(8,128)} %copy-done.2) | copy-start | bytes 3145732
  113.0 19.7 %collective-permute-start.18 = (f32[1,512]{1,0:T(1,128)S(1)}, f32[1,512]{1,0:T(1,128)S(1)}, u32[]{:S(2)}, u32[]{:S(2)}) collective-permute-start(f32[1,512]{1,0:T(1,128)S(1)} %shard_map.131.one_ref), channel_id=1, source_target_pairs={{0,496},{16,480},{32,464},{48,448},{64,432},{80,416},{96,400},{112... | collective-permute-start | bytes 6152 | tf_op jit(solution)/shard_map/ppermute | solution.py:259
  (4 other events, 14.1 us)
